TPU v7x, 32 devices: a whole 2x2x4 slice. The times are simulated.
32 devices in a mesh: ctx: 8 (over y, x, core), wa: 4 (over z).
Axes of the slice: x: 2, y: 2, z: 4, core: 2. Of those that a mesh axis runs over, the one named last changes fastest.
Arguments:
- hidden: bfloat16 [4, 2048, 512], P('wa', 'ctx'), may hold values from -6 to 6
- stream: bfloat16 [4, 2048, 512], P('wa', 'ctx'), may hold values from -6 to 6
- encoder: bfloat16 [4, 2048, 512], P('wa', 'ctx'), may hold values from -6 to 6
- lengths: int32 [4, 4], P('wa'), may hold values from 1 to 1024, 2048 in all within a row
- order: int32 [4, 2048], P('wa'), may hold values from 0 to 2047, each once within a row
- ranks: int32 [4, 2048], P('wa'), may hold values from 0 to 1023
- thresholds: int32 [4, 2048], P('wa'), may hold values from 1 to 1024
- self_query: bfloat16 [512, 512], P('wa'), may hold values from -0.25 to 0.25
- self_key_value: bfloat16 [512, 1024], P('wa'), may hold values from -0.25 to 0.25
- self_output: bfloat16 [512, 512], P('wa'), may hold values from -1 to 1
- cross_query: bfloat16 [512, 512], P('wa'), may hold values from -0.25 to 0.25
- cross_key_value: bfloat16 [512, 1024], P('wa'), may hold values from -0.25 to 0.25
- cross_output: bfloat16 [512, 512], P('wa'), may hold values from -1 to 1
- ffn_in: bfloat16 [512, 2048], P('wa'), may hold values from -0.25 to 0.25
- ffn_out: bfloat16 [2048, 512], P('wa'), may hold values from -0.1875 to 0.1875
- norm_gain: bfloat16 [3, 512], P(None, 'wa'), may hold values from 0.5 to 1.5
- norm_shift: bfloat16 [3, 512], P(None, 'wa'), may hold values from -2 to 2
- cotangent: bfloat16 [4, 2048, 512], P('wa', 'ctx'), may hold values from -6 to 6
Outputs:
- layer_out: bfloat16 [4, 2048, 512], P('wa', 'ctx')
- hidden_grad: float32 [4, 2048, 512], P('wa', 'ctx')
- stream_grad: float32 [4, 2048, 512], P('wa', 'ctx')
- encoder_grad: float32 [4, 2048, 512], P('wa', 'ctx')
- self_query_grad: float32 [512, 512], P('wa')
- self_key_value_grad: float32 [512, 1024], P('wa')
- self_output_grad: float32 [512, 512], P('wa')
- cross_query_grad: float32 [512, 512], P('wa')
- cross_key_value_grad: float32 [512, 1024], P('wa')
- cross_output_grad: float32 [512, 512], P('wa')
- ffn_in_grad: float32 [512, 2048], P('wa')
- ffn_out_grad: float32 [2048, 512], P('wa')
- norm_gain_grad: float32 [3, 512], P(None, 'wa')
- norm_shift_grad: float32 [3, 512], P(None, 'wa')
All inputs are finite; a program needn't handle non-finite values.
Results may differ from a plain program's by a relative error of at most 0.022.
Values may be sent and summed in bfloat16 or wider, within the bound.
No kernel may reach another device: no remote copies, remote signals or barrier semaphores. Data moves between devices by JAX's collectives and lax.ppermute only.
A program may use at most 384 MiB of HBM per device.

v0:
```python
import functools

import jax
import jax.numpy as jnp
from jax import lax
from jax.experimental import pallas as pl
from jax.experimental.pallas import tpu as pltpu
from jax.sharding import Mesh
from jax.sharding import PartitionSpec as P

D = 512
HEADS = 8
HEAD = 64
KEYBLK = 1024


layer_eps = 1e-05
neg_fill = -1e30


def sequence_ids(positions, seq_ends):
    return jnp.sum((positions[:, None] >= seq_ends[None, :]).astype(jnp.int32), axis=1)


def head_split(matrix):
    return matrix.reshape(matrix.shape[0], HEADS, HEAD)


def block_scores(query_heads, key_heads):
    raw_scores = jnp.einsum(
        "lhd,khd->hlk", query_heads, key_heads, preferred_element_type=jnp.float32
    )
    return raw_scores * float(HEAD) ** (-0.5)


def softmax_totals(queries, key_rows, allowed_fn):
    query_heads = head_split(queries)
    count_rows = queries.shape[0]

    def visit(state_pair, block_index):
        running_top, running_sum = state_pair
        block_start = block_index * KEYBLK
        key_piece = lax.dynamic_slice_in_dim(key_rows, block_start, KEYBLK, 0)
        allowed = allowed_fn(block_start)[None]
        scores = jnp.where(
            allowed, block_scores(query_heads, head_split(key_piece[:, :D])), neg_fill
        )
        new_top = jnp.maximum(running_top, jnp.max(scores, axis=2))
        weights = jnp.where(allowed, jnp.exp(scores - new_top[:, :, None]), 0.0)
        running_sum = running_sum * jnp.exp(running_top - new_top) + jnp.sum(weights, axis=2)
        return ((new_top, running_sum), None)

    initial = (
        jnp.full((HEADS, count_rows), neg_fill, jnp.float32),
        jnp.zeros((HEADS, count_rows), jnp.float32),
    )
    (final_top, final_sum), unused = lax.scan(
        visit, initial, jnp.arange(key_rows.shape[0] // KEYBLK)
    )
    return final_top + jnp.log(final_sum)


def attend_values(queries, key_rows, log_totals, allowed_fn):
    query_heads = head_split(queries)

    def visit(running, block_index):
        block_start = block_index * KEYBLK
        key_piece = lax.dynamic_slice_in_dim(key_rows, block_start, KEYBLK, 0)
        allowed = allowed_fn(block_start)[None]
        scores = block_scores(query_heads, head_split(key_piece[:, :D]))
        weights = jnp.where(allowed, jnp.exp(scores - log_totals[:, :, None]), 0.0)
        value_heads = head_split(key_piece[:, D:])
        return (
            running
            + jnp.einsum(
                "hlk,khd->lhd",
                weights.astype(jnp.bfloat16),
                value_heads,
                preferred_element_type=jnp.float32,
            ),
            None,
        )

    mixed, unused = lax.scan(
        visit, jnp.zeros(query_heads.shape, jnp.float32), jnp.arange(key_rows.shape[0] // KEYBLK)
    )
    return mixed.reshape(queries.shape[0], D)


def head_offsets(grad_low, attended):
    return jnp.sum(head_split(grad_low.astype(jnp.float32) * attended), axis=2).T


def attend_back(queries, key_rows, log_totals, attended, grad_low, allowed_fn):
    query_heads = head_split(queries)
    grad_heads = head_split(grad_low)
    offsets = head_offsets(grad_low, attended)
    scale_value = float(HEAD) ** (-0.5)

    def visit(query_grad, block_index):
        block_start = block_index * KEYBLK
        key_piece = lax.dynamic_slice_in_dim(key_rows, block_start, KEYBLK, 0)
        allowed = allowed_fn(block_start)[None]
        key_heads = head_split(key_piece[:, :D])
        value_heads = head_split(key_piece[:, D:])
        weights = jnp.where(
            allowed, jnp.exp(block_scores(query_heads, key_heads) - log_totals[:, :, None]), 0.0
        )
        value_grad = jnp.einsum(
            "hlk,lhd->khd",
            weights.astype(jnp.bfloat16),
            grad_heads,
            preferred_element_type=jnp.float32,
        )
        weight_grad = jnp.einsum(
            "lhd,khd->hlk", grad_heads, value_heads, preferred_element_type=jnp.float32
        )
        score_grad = (weights * (weight_grad - offsets[:, :, None]) * scale_value).astype(
            jnp.bfloat16
        )
        query_grad = query_grad + jnp.einsum(
            "hlk,khd->lhd", score_grad, key_heads, preferred_element_type=jnp.float32
        )
        key_grad = jnp.einsum(
            "hlk,lhd->khd", score_grad, query_heads, preferred_element_type=jnp.float32
        )
        return (
            query_grad,
            jnp.concatenate((key_grad.reshape(KEYBLK, D), value_grad.reshape(KEYBLK, D)), axis=1),
        )

    query_grad, grad_pieces = lax.scan(
        visit, jnp.zeros(query_heads.shape, jnp.float32), jnp.arange(key_rows.shape[0] // KEYBLK)
    )
    return (query_grad.reshape(queries.shape[0], D), grad_pieces.reshape(key_rows.shape[0], 2 * D))


def normalize(values, gain_row, shift_row):
    row_mean = jnp.mean(values, axis=1, keepdims=True)
    centred = values - row_mean
    scale_inv = lax.rsqrt(jnp.mean(centred * centred, axis=1, keepdims=True) + layer_eps)
    normed = centred * scale_inv
    return (normed * gain_row + shift_row, normed, scale_inv)


def normalize_back(grad_out, normed, scale_inv, gain_row):
    gain_term = jnp.sum(grad_out * normed, axis=0)
    shift_term = jnp.sum(grad_out, axis=0)
    scaled = grad_out * gain_row
    grad_in = scale_inv * (
        scaled
        - jnp.mean(scaled, axis=1, keepdims=True)
        - normed * jnp.mean(scaled * normed, axis=1, keepdims=True)
    )
    return (grad_in, gain_term, shift_term)


def matmul(left, right):
    return jnp.dot(left, right, preferred_element_type=jnp.float32)


def general_shards(
    hidden,
    stream,
    encoder,
    lengths,
    order,
    ranks,
    thresholds,
    self_query,
    self_key_value,
    self_output,
    cross_query,
    cross_key_value,
    cross_output,
    ffn_in,
    ffn_out,
    norm_gain,
    norm_shift,
    cotangent,
):
    (
        full_query,
        full_pair,
        full_output,
        full_cross_query,
        full_cross_pair,
        full_cross_output,
        full_in,
        full_out,
        gain_rows,
        shift_rows,
    ) = (
        lax.all_gather(self_query, "wa", axis=0, tiled=True),
        lax.all_gather(self_key_value, "wa", axis=0, tiled=True),
        lax.all_gather(self_output, "wa", axis=0, tiled=True),
        lax.all_gather(cross_query, "wa", axis=0, tiled=True),
        lax.all_gather(cross_key_value, "wa", axis=0, tiled=True),
        lax.all_gather(cross_output, "wa", axis=0, tiled=True),
        lax.all_gather(ffn_in, "wa", axis=0, tiled=True),
        lax.all_gather(ffn_out, "wa", axis=0, tiled=True),
        lax.all_gather(norm_gain, "wa", axis=1, tiled=True),
        lax.all_gather(norm_shift, "wa", axis=1, tiled=True),
    )
    gains = gain_rows.astype(jnp.float32)
    shifts = shift_rows.astype(jnp.float32)
    local_rows = hidden.shape[1]
    total_rows = order.shape[1]
    row_start = lax.axis_index("ctx") * local_rows
    seq_ends = jnp.cumsum(lengths[0])
    token_seq = sequence_ids(order[0], seq_ends)
    source_seq = sequence_ids(jnp.arange(total_rows, dtype=jnp.int32), seq_ends)
    query_seq = lax.dynamic_slice_in_dim(token_seq, row_start, local_rows)
    query_rows = row_start + jnp.arange(local_rows, dtype=jnp.int32)
    all_limits = thresholds[0]
    limits = lax.dynamic_slice_in_dim(all_limits, row_start, local_rows)
    key_ranks = ranks[0]

    def self_allowed(block_start):
        block_seq = lax.dynamic_slice_in_dim(token_seq, block_start, KEYBLK)
        block_rank = lax.dynamic_slice_in_dim(key_ranks, block_start, KEYBLK)
        block_rows = block_start + jnp.arange(KEYBLK, dtype=jnp.int32)
        return (query_seq[:, None] == block_seq[None, :]) & (
            (block_rank[None, :] < limits[:, None]) | (query_rows[:, None] == block_rows[None, :])
        )

    def cross_allowed(block_start):
        return (
            query_seq[:, None] == lax.dynamic_slice_in_dim(source_seq, block_start, KEYBLK)[None, :]
        )

    inputs = hidden[0]
    stream_rows = stream[0]
    source_rows = encoder[0]
    queries = matmul(inputs, full_query).astype(jnp.bfloat16)
    self_local = matmul(stream_rows, full_pair).astype(jnp.bfloat16)
    cross_local = matmul(source_rows, full_cross_pair).astype(jnp.bfloat16)
    self_keys, cross_keys = (
        lax.all_gather(self_local, "ctx", axis=0, tiled=True),
        lax.all_gather(cross_local, "ctx", axis=0, tiled=True),
    )
    self_totals = softmax_totals(queries, self_keys, self_allowed)
    self_mixed = attend_values(queries, self_keys, self_totals, self_allowed)
    self_low = self_mixed.astype(jnp.bfloat16)
    first, first_normed, first_scale = normalize(
        inputs.astype(jnp.float32) + matmul(self_low, full_output), gains[0], shifts[0]
    )
    first_low = first.astype(jnp.bfloat16)
    cross_queries = matmul(first_low, full_cross_query).astype(jnp.bfloat16)
    cross_totals = softmax_totals(cross_queries, cross_keys, cross_allowed)
    cross_mixed = attend_values(cross_queries, cross_keys, cross_totals, cross_allowed)
    cross_low = cross_mixed.astype(jnp.bfloat16)
    second, second_normed, second_scale = normalize(
        first + matmul(cross_low, full_cross_output), gains[1], shifts[1]
    )
    second_low = second.astype(jnp.bfloat16)
    hidden_pre = matmul(second_low, full_in)
    sigmoid_pre = jax.nn.sigmoid(hidden_pre)
    activated = (hidden_pre * sigmoid_pre).astype(jnp.bfloat16)
    result, third_normed, third_scale = normalize(
        second + matmul(activated, full_out), gains[2], shifts[2]
    )
    third_grad, gain_grad_c, shift_grad_c = normalize_back(
        cotangent[0].astype(jnp.float32), third_normed, third_scale, gains[2]
    )
    branch_grad = third_grad.astype(jnp.bfloat16)
    grad_ffn_out = matmul(activated.T, branch_grad)
    slope = sigmoid_pre * (1.0 + hidden_pre * (1.0 - sigmoid_pre))
    pre_grad = (matmul(branch_grad, full_out.T) * slope).astype(jnp.bfloat16)
    grad_ffn_in = matmul(second_low.T, pre_grad)
    second_total = third_grad + matmul(pre_grad, full_in.T)
    second_grad, gain_grad_b, shift_grad_b = normalize_back(
        second_total, second_normed, second_scale, gains[1]
    )
    cross_branch = second_grad.astype(jnp.bfloat16)
    grad_cross_output = matmul(cross_low.T, cross_branch)
    cross_mixed_grad = matmul(cross_branch, full_cross_output.T).astype(jnp.bfloat16)
    cross_query_term, cross_terms = attend_back(
        cross_queries, cross_keys, cross_totals, cross_mixed, cross_mixed_grad, cross_allowed
    )
    cross_query_low = cross_query_term.astype(jnp.bfloat16)
    grad_cross_query = matmul(first_low.T, cross_query_low)
    first_total = second_grad + matmul(cross_query_low, full_cross_query.T)
    first_grad, gain_grad_a, shift_grad_a = normalize_back(
        first_total, first_normed, first_scale, gains[0]
    )
    self_branch = first_grad.astype(jnp.bfloat16)
    grad_self_output = matmul(self_low.T, self_branch)
    self_mixed_grad = matmul(self_branch, full_output.T).astype(jnp.bfloat16)
    self_query_term, self_terms = attend_back(
        queries, self_keys, self_totals, self_mixed, self_mixed_grad, self_allowed
    )
    self_sum, cross_sum = (
        lax.psum_scatter(self_terms, "ctx", scatter_dimension=0, tiled=True),
        lax.psum_scatter(cross_terms, "ctx", scatter_dimension=0, tiled=True),
    )
    self_query_low = self_query_term.astype(jnp.bfloat16)
    grad_self_query = matmul(inputs.T, self_query_low)
    input_grad = first_grad + matmul(self_query_low, full_query.T)
    self_sum_low = self_sum.astype(jnp.bfloat16)
    grad_self_pair = matmul(stream_rows.T, self_sum_low)
    stream_grad = matmul(self_sum_low, full_pair.T)
    cross_sum_low = cross_sum.astype(jnp.bfloat16)
    grad_cross_pair = matmul(source_rows.T, cross_sum_low)
    source_grad = matmul(cross_sum_low, full_cross_pair.T)
    gain_grads = jnp.stack((gain_grad_a, gain_grad_b, gain_grad_c))
    shift_grads = jnp.stack((shift_grad_a, shift_grad_b, shift_grad_c))
    (
        share_query,
        share_pair,
        share_output,
        share_cross_query,
        share_cross_pair,
        share_cross_output,
        share_in,
        share_out,
        share_gain,
        share_shift,
    ) = (
        lax.psum_scatter(
            grad_self_query.astype(jnp.bfloat16), "wa", scatter_dimension=0, tiled=True
        ).astype(jnp.float32),
        lax.psum_scatter(
            grad_self_pair.astype(jnp.bfloat16), "wa", scatter_dimension=0, tiled=True
        ).astype(jnp.float32),
        lax.psum_scatter(
            grad_self_output.astype(jnp.bfloat16), "wa", scatter_dimension=0, tiled=True
        ).astype(jnp.float32),
        lax.psum_scatter(
            grad_cross_query.astype(jnp.bfloat16), "wa", scatter_dimension=0, tiled=True
        ).astype(jnp.float32),
        lax.psum_scatter(
            grad_cross_pair.astype(jnp.bfloat16), "wa", scatter_dimension=0, tiled=True
        ).astype(jnp.float32),
        lax.psum_scatter(
            grad_cross_output.astype(jnp.bfloat16), "wa", scatter_dimension=0, tiled=True
        ).astype(jnp.float32),
        lax.psum_scatter(
            grad_ffn_in.astype(jnp.bfloat16), "wa", scatter_dimension=0, tiled=True
        ).astype(jnp.float32),
        lax.psum_scatter(
            grad_ffn_out.astype(jnp.bfloat16), "wa", scatter_dimension=0, tiled=True
        ).astype(jnp.float32),
        lax.psum_scatter(
            gain_grads.astype(jnp.bfloat16), "wa", scatter_dimension=1, tiled=True
        ).astype(jnp.float32),
        lax.psum_scatter(
            shift_grads.astype(jnp.bfloat16), "wa", scatter_dimension=1, tiled=True
        ).astype(jnp.float32),
    )
    (
        total_query,
        total_pair,
        total_output,
        total_cross_query,
        total_cross_pair,
        total_cross_output,
        total_in,
        total_out,
        total_gain,
        total_shift,
    ) = lax.psum(
        (
            share_query,
            share_pair,
            share_output,
            share_cross_query,
            share_cross_pair,
            share_cross_output,
            share_in,
            share_out,
            share_gain,
            share_shift,
        ),
        "ctx",
    )
    return (
        result.astype(jnp.bfloat16)[None],
        input_grad[None],
        stream_grad[None],
        source_grad[None],
        total_query,
        total_pair,
        total_output,
        total_cross_query,
        total_cross_pair,
        total_cross_output,
        total_in,
        total_out,
        total_gain,
        total_shift,
    )


PAIR = 2 * HEAD
PAIRS = HEADS // 2
FF = 2048
low_t = jnp.bfloat16
wide_t = jnp.float32
vmem_spec = pl.BlockSpec(memory_space=pltpu.VMEM)
smem_spec = pl.BlockSpec(memory_space=pltpu.SMEM)


def run(body, outs, ids, args, scratch=(), us=2, vmem=56):
    outs = [jax.ShapeDtypeStruct(shape, kind) for shape, kind in outs]
    arrays = [arg[0] if isinstance(arg, tuple) else arg for arg in args]
    parts = [n for n, arg in enumerate(args) if isinstance(arg, tuple)]
    total = len(args) + len(outs) + len(scratch)

    def kernel(ids, *refs):
        refs, buffers, sems = list(refs[:total]), refs[total:-1], refs[-1]
        copies = []
        for m, n in enumerate(parts):
            start = args[n][1] * D
            copies.append(
                pltpu.make_async_copy(refs[n].at[:, :, start : start + D], buffers[m], sems.at[m])
            )
            copies[m].start()
            refs[n] = buffers[m]
        for copy in copies:
            copy.wait()
        body(ids, *refs)

    buffers = [pltpu.VMEM(args[n][0].shape[:2] + (D,), args[n][0].dtype) for n in parts]
    specs = [pl.BlockSpec(memory_space=pl.ANY) if n in parts else vmem_spec for n in range(len(args))]
    moved = sum(a.size * a.dtype.itemsize for a in arrays + outs)
    return pl.pallas_call(
        kernel,
        name=getattr(body, "func", body).__name__,
        out_shape=outs,
        in_specs=[smem_spec] + specs,
        out_specs=[vmem_spec] * len(outs),
        scratch_shapes=[pltpu.VMEM(shape, kind) for shape, kind in scratch]
        + buffers
        + [pltpu.SemaphoreType.DMA((max(1, len(parts)),))],
        compiler_params=pltpu.CompilerParams(vmem_limit_bytes=vmem * 1024 * 1024),
        cost_estimate=pl.CostEstimate(flops=us * 1_000_000_000, bytes_accessed=moved, transcendentals=0),
    )(ids, *arrays)


def dot_nn(a, b):
    return lax.dot_general(a, b, (((1,), (0,)), ((), ())), preferred_element_type=wide_t)


def dot_nt(a, b):
    return lax.dot_general(a, b, (((1,), (1,)), ((), ())), preferred_element_type=wide_t)


def dot_tn(a, b):
    return lax.dot_general(a, b, (((0,), (0,)), ((), ())), preferred_element_type=wide_t)


def at16(start, size=16):
    return pl.ds(pl.multiple_of(start, 16), size)


def at128(start, size=128):
    return pl.ds(pl.multiple_of(start, 128), size)


def half_mask(shape, axis, core):
    return (lax.broadcasted_iota(jnp.int32, shape, axis) // HEAD) == core


def attend_rows(q_ref, k_ref, vt_ref, bias_ref, s_ref, ot_ref, lse_ref):
    keys, rows = bias_ref.shape
    tile = min(1024, keys)
    spans = [slice(start, start + tile) for start in range(0, keys, tile)]
    lowest = jnp.full((8, rows), neg_fill, wide_t)
    group = 4

    def step(p, carry):
        def scores(head, here, top):
            pair = at128((p * (group // 2) + head // 2) * PAIR)
            q = q_ref[:, pair]
            own_q = jnp.where(half_mask((rows, PAIR), 1, head % 2), q, jnp.zeros_like(q))
            s = dot_nt(k_ref[here, pair], own_q) + bias_ref[here, :]
            s_ref[head % 2, here, :] = s
            return jnp.maximum(top, jnp.max(s.reshape(tile // 8, 8, rows), axis=0))

        top = lowest
        for here in spans:
            top = scores(0, here, top)
        for head in range(group):
            features = pl.ds(pl.multiple_of((p * group + head) * HEAD, HEAD), HEAD)
            highest = jnp.max(top, axis=0, keepdims=True)
            total = jnp.zeros((8, rows), wide_t)
            mixed = jnp.zeros((HEAD, rows), wide_t)
            top = lowest
            for here in spans:
                if head + 1 < group:
                    top = scores(head + 1, here, top)
                w = jnp.exp(s_ref[head % 2, here, :] - highest)
                total = total + jnp.sum(w.reshape(tile // 8, 8, rows), axis=0)
                mixed = mixed + dot_nn(vt_ref[features, here], w.astype(low_t))
            total = jnp.sum(total, axis=0, keepdims=True)
            ot_ref[features, :] = mixed / total
            lse_ref[pl.ds(p * group + head, 1), :] = highest + jnp.log(total)
        return carry

    lax.fori_loop(0, HEADS // group, step, 0)


def finish_rows(ot_ref, low_out, mixed_out):
    mixed = ot_ref[...].T
    low_out[...] = mixed.astype(low_t)
    mixed_out[...] = mixed


def three_parts(value):
    high = value.astype(low_t).astype(wide_t)
    rest = value - high
    middle = rest.astype(low_t).astype(wide_t)
    return high, middle, rest - middle


def side_rows(lse, grad_low, mixed, row_data):
    product = grad_low.astype(wide_t) * mixed[...]
    lane = lax.broadcasted_iota(jnp.int32, (grad_low.shape[0], PAIR), 1)
    sums = jnp.zeros((grad_low.shape[0], PAIR), wide_t)
    for p in range(PAIRS):
        piece = product[:, p * PAIR : (p + 1) * PAIR]
        for h in range(2):
            mine = half_mask(piece.shape, 1, h)
            offset = jnp.sum(jnp.where(mine, piece, 0.0), axis=1, keepdims=True)
            sums = jnp.where(lane == p * 2 + h, offset, sums)
    offsets = sums.T
    seq = row_data[16:17, :]
    onehot = [(seq == float(n)).astype(wide_t) for n in range(4)]
    sides = []
    for p in range(PAIRS):
        pieces = []
        for h in range(2):
            head = p * 2 + h
            pieces += three_parts(-lse[head : head + 1, :])
            pieces += three_parts(-offsets[head : head + 1, :])
        sides.append(jnp.concatenate(pieces + onehot, axis=0).astype(low_t))
    return sides


def side_lanes(side, core):
    side = side.astype(wide_t)
    head = jnp.where(core == 0, side[0:6], side[6:12])
    gap = jnp.zeros((5, side.shape[1]), wide_t)
    rest = jnp.zeros((HEAD - 20, side.shape[1]), wide_t)
    half = jnp.concatenate((head[0:3], gap, head[3:6], gap, side[12:16], rest), axis=0)
    return jnp.concatenate((half, half), axis=0).T.astype(low_t)


def assemble(ids, parts, column, outs):
    for chip, other, block in parts:
        own = chip * 2 + (ids[1] ^ other)
        for e in range(4):
            rows = at16((ids[2] ^ e) * 128 + own * 16)
            start = column
            for out in outs:
                width = out.shape[1]
                out[rows, :] = block[e * 16 : (e + 1) * 16, start : start + width]
                start += width


def project_pairs(parts, w_pair, k_ref, vt_ref, wvt_ref):
    wvt_ref[...] = w_pair[:, D:].astype(wide_t).T.astype(low_t)
    for n, part in enumerate(parts):
        for k in range(PAIRS):
            rows = part.shape[1]
            start = (n * 4 + k) * rows
            k_ref[start : start + rows, :] = dot_nn(part[k], w_pair[:, :D]).astype(low_t)
            vt_ref[:, start : start + rows] = dot_nt(wvt_ref[...], part[k]).astype(low_t)


def self_forward(ids, hidden, own, other, *refs):
    slices, (cols, row_data), refs = refs[:8], refs[8:10], refs[10:]
    out, mixed, lse, wq, wkv, q_ref, k_ref, vt_ref, wvt_ref, bias_ref, s_ref, ot_ref = refs
    rows = hidden.shape[0]
    parts = [(ids[0] ^ k, n, slices[n * 4 + k]) for n in range(2) for k in range(4)]
    assemble(ids, parts, 0, (wq, wkv))
    q_ref[...] = (dot_nn(hidden[...], wq[...]).astype(low_t) * 0.125).astype(low_t)
    project_pairs((own, other), wkv, k_ref, vt_ref, wvt_ref)
    seq, limit = row_data[16:17, :], row_data[17:18, :]
    for b in range(8):
        seen = (cols[:, b : b + 1] == seq) & (cols[:, 8 + b : 9 + b] < limit)
        bias_ref[b * rows : (b + 1) * rows, :] = jnp.where(seen, 0.0, neg_fill)
    mine = lax.broadcasted_iota(jnp.int32, (rows, rows), 0) == lax.broadcasted_iota(
        jnp.int32, (rows, rows), 1
    )
    block = at128(ids[0] * rows, rows)
    bias_ref[block, :] = jnp.where(mine, 0.0, bias_ref[block, :])
    attend_rows(q_ref, k_ref, vt_ref, bias_ref, s_ref, ot_ref, lse)
    finish_rows(ot_ref, out, mixed)


def layer_norm(values, gain_row, shift_row):
    mean = jnp.mean(values, axis=1, keepdims=True)
    centred = values - mean
    scale = lax.rsqrt(jnp.mean(centred * centred, axis=1, keepdims=True) + layer_eps)
    normed = centred * scale
    return normed * gain_row + shift_row, normed, scale


def layer_norm_back(grad, normed, scale, gain_row):
    gain_term = jnp.sum(grad * normed, axis=0, keepdims=True)
    shift_term = jnp.sum(grad, axis=0, keepdims=True)
    scaled = grad * gain_row
    grad_in = scale * (
        scaled
        - jnp.mean(scaled, axis=1, keepdims=True)
        - normed * jnp.mean(scaled * normed, axis=1, keepdims=True)
    )
    return grad_in, gain_term, shift_term


def head_arrays(ids, k_ref, vt_ref, cols, column, k_all, v_all, kt, turn):
    rows = turn.shape[1]
    core = ids[1]
    mine = half_mask((rows, PAIR), 1, core)
    features = pl.ds(pl.multiple_of(core * HEAD, HEAD), HEAD)
    lane = lax.broadcasted_iota(jnp.int32, (rows, PAIR), 1) % HEAD
    ones_v = jnp.where((lane >= 8) & (lane < 11), 1.0, 0.0).astype(low_t)
    pair = at128(ids[0] * PAIR)
    for b in range(8):
        here = slice(b * rows, (b + 1) * rows)
        seq = cols[:, column + b : column + b + 1].astype(jnp.int32)
        other_seq = (lane >= 16) & (lane < 20) & (lane != seq + 16)
        ones_k = jnp.where(other_seq, neg_fill, jnp.where(lane < 3, 1.0, 0.0)).astype(low_t)
        key = k_ref[here, pair]
        k_all[here, :] = jnp.where(mine, key, ones_k)
        turn[...] = key.astype(wide_t).T
        kt[:, here] = turn[features, :].astype(low_t)
        v_all[here, :] = jnp.where(mine, turned(vt_ref[pair, here]), ones_v)


def cross_forward(ids, hidden, self_low, own, other, *refs):
    slices, (cols, row_data) = refs[:2], refs[2:4]
    first, normed, scale_out, first_low, cross_low, mixed, lse, cross_q = refs[4:12]
    wo, wcq, wckv, wco, gs, k_all, v_all, kt = refs[12:20]
    q_ref, k_ref, vt_ref, wvt_ref, bias_ref, s_ref, ot_ref, turn = refs[20:]
    for n in range(2):
        for e in range(4):
            rows = at16(e * 128 + (ids[1] ^ n) * 64, 64)
            start = 0
            for out in (wo, wcq, wckv, wco):
                width = out.shape[1]
                out[rows, :] = slices[n][e, :, start : start + width]
                start += width
    for e in range(4):
        gs[:, e * 128 : (e + 1) * 128] = slices[0][e, :16, 5 * D :]
    gain, shift = gs[0:1, :].astype(wide_t), gs[3:4, :].astype(wide_t)
    value, n0, s0 = layer_norm(
        hidden[...].astype(wide_t) + dot_nn(self_low[...], wo[...]), gain, shift
    )
    first[...] = value
    normed[...] = n0
    scale_out[...] = jnp.broadcast_to(s0, scale_out.shape)
    low = value.astype(low_t)
    first_low[...] = low
    q = dot_nn(low, wcq[...]).astype(low_t)
    cross_q[...] = q
    q_ref[...] = (q * 0.125).astype(low_t)
    rows = hidden.shape[0]
    project_pairs((own, other), wckv, k_ref, vt_ref, wvt_ref)
    for b in range(8):
        seen = cols[:, 16 + b : 17 + b] == row_data[16:17, :]
        bias_ref[b * rows : (b + 1) * rows, :] = jnp.where(seen, 0.0, neg_fill)
    attend_rows(q_ref, k_ref, vt_ref, bias_ref, s_ref, ot_ref, lse)
    finish_rows(ot_ref, cross_low, mixed)
    head_arrays(ids, k_ref, vt_ref, cols, 16, k_all, v_all, kt, turn)


def feed_forward(ids, first, cross_low, cross_mixed, lse, row_data, cross_q, wco, gs, cotangent, *refs):
    slices = refs[0:8]
    result, dealt, second_grad, keep, send, sums, slope, wins, wouts = refs[8:]
    half_ff = FF // 2
    for n in range(2):
        for k in range(4):
            chip, core, part = ids[0] ^ k, ids[1] ^ n, slices[n * 4 + k]
            for e in range(4):
                w, here = ids[2] ^ e, slice(e * 16, (e + 1) * 16)
                rows = at16(w * 128 + (chip * 2 + core) * 16)
                for g in range(4):
                    row = w * 256 + ((chip % 2) * 2 + core) * 64 + g * 16
                    wouts[(chip // 2) ^ ids[1], at16(row), :] = part[here, FF + g * D : FF + (g + 1) * D]
                    for h in range(2):
                        column = g * 512 + h * 256
                        wins[h ^ ids[1], rows, g * 256 : (g + 1) * 256] = part[here, column : column + 256]
    gains, shifts = gs[0:3, :].astype(wide_t), gs[3:6, :].astype(wide_t)
    second, n1, s1 = layer_norm(
        first[...] + dot_nn(cross_low[...], wco[...]), gains[1:2], shifts[1:2]
    )
    low = second.astype(low_t)
    for out in (keep, send):
        out[:, 2 * half_ff : 2 * half_ff + D] = low
        out[:, 2 * half_ff + 2 * D : 2 * half_ff + 3 * D] = cross_low[...]
    width = 512
    chunks = [(n, c) for n in range(2) for c in range(FF // 2 // width)]
    total = second
    for n, c in chunks:
        here = slice(c * width, (c + 1) * width)
        wide = slice(n * half_ff + c * width, n * half_ff + (c + 1) * width)
        pre = dot_nn(low, wins[n, :, here])
        sig = 1.0 / (1.0 + jnp.exp(-pre))
        act = (pre * sig).astype(low_t)
        (keep, send)[n][:, half_ff + c * width : half_ff + (c + 1) * width] = act
        slope[:, wide] = sig * (1.0 + pre * (1.0 - sig))
        total = total + dot_nn(act, wouts[n, here, :])
    value, n2, s2 = layer_norm(total, gains[2:3], shifts[2:3])
    result[...] = value.astype(low_t)
    third, gain_c, shift_c = layer_norm_back(cotangent[...].astype(wide_t), n2, s2, gains[2:3])
    third_low = third.astype(low_t)
    for out in (keep, send):
        out[:, 2 * half_ff + D : 2 * half_ff + 2 * D] = third_low
    total = third
    for n, c in chunks:
        here = slice(c * width, (c + 1) * width)
        wide = slice(n * half_ff + c * width, n * half_ff + (c + 1) * width)
        back = (dot_nt(third_low, wouts[n, here, :]) * slope[:, wide]).astype(low_t)
        (keep, send)[n][:, here] = back
        total = total + dot_nt(back, wins[n, :, here])
    grad, gain_b, shift_b = layer_norm_back(total, n1, s1, gains[1:2])
    second_grad[...] = grad
    grad_low = grad.astype(low_t)
    for out, core in ((keep, ids[1]), (send, 1 - ids[1])):
        half = grad_low[:, : D // 2]
        out[:, 2 * half_ff + 3 * D :] = jnp.where(core == 0, half, grad_low[:, D // 2 :])
    mixed = dot_nt(grad_low, wco[...]).astype(low_t)
    rows = grad_low.shape[0]
    sides = side_rows(lse, mixed, cross_mixed, row_data)
    for p in range(PAIRS):
        dealt[p, :rows, :PAIR] = cross_q[:, p * PAIR : (p + 1) * PAIR]
        dealt[p, :rows, PAIR:] = mixed[:, p * PAIR : (p + 1) * PAIR]
        dealt[p, rows:, :] = sides[p]
    zero = jnp.zeros_like(gain_b)
    sums[...] = jnp.concatenate((zero, gain_b, gain_c, zero, shift_b, shift_c, zero, zero), axis=0)


def grads_a(ids, keep, received, out, g_in, g_out, g_cross):
    half = FF // 2

    def both(left, right):
        return (dot_tn(keep[:, left], keep[:, right]) + dot_tn(received[:, left], received[:, right])).astype(low_t)

    at = [0, half] + [2 * half + n * D for n in range(4)]
    pre, act = slice(at[0], at[1]), slice(at[1], at[2])
    second, branch, low = (slice(at[n], at[n] + D) for n in (2, 3, 4))
    g_in[...] = both(second, pre)
    g_out[...] = both(act, branch)
    g_cross[...] = both(low, slice(at[5], at[5] + D // 2))
    for chip in range(4):
        for e in range(4):
            w, here = ids[2] ^ e, slice(e * 32, (e + 1) * 32)
            rows = at16(w * 128 + chip * 32, 32)
            out[chip, here, :half] = g_in[rows, :]
            for g in range(2):
                out[chip, here, half + g * D : half + (g + 1) * D] = g_out[
                    at16(w * 256 + chip * 64 + g * 32, 32), :
                ]
            out[chip, here, half + 2 * D :] = g_cross[rows, :]


def grads_b(ids, first_low, cross_dq, self_low, branch, sums, dkv, out, g_query, g_output):
    g_query[...] = dot_tn(first_low[...], cross_dq[...]).astype(low_t)
    g_output[...] = dot_tn(self_low[...], branch[...]).astype(low_t)
    row = jnp.concatenate((sums[...], jnp.zeros_like(sums[...])), axis=0).astype(low_t)
    rows = dkv.shape[2]
    for e in range(4):
        w, here = ids[2] ^ e, slice(e * 16, (e + 1) * 16)
        piece = row[:, :128]
        for k in range(1, 4):
            piece = jnp.where(w == k, row[:, k * 128 : (k + 1) * 128], piece)
        for device in range(8):
            own = at16(w * 128 + device * 16)
            out[device, here, :D] = g_query[own, :]
            out[device, here, D : 2 * D] = g_output[own, :]
            out[device, here, 2 * D : 2 * D + 128] = piece
    for device in range(8):
        for n in range(2):
            start = 2 * D + 128 + n * rows
            out[device, :, start : start + rows] = dkv[device, n * HEAD : (n + 1) * HEAD, :]


def pair_setup(is_self, ids, own, other, w_pair, cols, *refs):
    k_all, v_all, kt, turn = refs
    chip, core = ids[0], ids[1]
    rows = own.shape[1]
    mine = half_mask((rows, PAIR), 1, core)
    features = pl.ds(pl.multiple_of(core * HEAD, HEAD), HEAD)
    lane = lax.broadcasted_iota(jnp.int32, (rows, PAIR), 1) % HEAD
    ones_v = jnp.where((lane >= 8) & (lane < 11), 1.0, 0.0).astype(low_t)
    pair = at128(chip * PAIR)
    wk, wv = w_pair[:, pair], w_pair[:, at128(D + chip * PAIR)]
    for n, part in enumerate((own, other)):
        for k in range(4):
            b = n * 4 + k
            here = slice(b * rows, (b + 1) * rows)
            column = b if is_self else 16 + b
            seq = cols[:, column : column + 1].astype(jnp.int32)
            other_seq = (lane >= 16) & (lane < 20) & (lane != seq + 16)
            ones_k = jnp.where(other_seq, neg_fill, jnp.where(lane < 3, 1.0, 0.0)).astype(low_t)
            key = dot_nn(part[k], wk)
            turn[...] = key.T
            kt[:, here] = turn[features, :].astype(low_t)
            k_all[here, :] = jnp.where(mine, key.astype(low_t), ones_k)
            v_all[here, :] = jnp.where(mine, dot_nn(part[k], wv).astype(low_t), ones_v)


def pair_queries(ids, own, other, w_query, q_all):
    wq = w_query[:, at128(ids[0] * PAIR)]
    for n, part in enumerate((own, other)):
        for k in range(4):
            q_all[n * 4 + k] = dot_nn(part[k], wq).astype(low_t)


def pair_back(is_self, ids, *refs):
    if is_self:
        q_parts, do_own, do_other, k_all, v_all, kt, cols, row_data, back = refs[:9]
        do_parts = (do_own, do_other)
    else:
        both_own, both_other, k_all, v_all, kt, dq_keep, dq_send, dkv = refs[:8]
        both_parts = (both_own, both_other)
    q_all, do_all, dq_t, dk, dv, rank, turn = refs[-7:]
    core = ids[1]
    rows = q_all.shape[1]
    keys = 8 * rows
    mine = half_mask((rows, PAIR), 1, core)
    features = pl.ds(pl.multiple_of(core * HEAD, HEAD), HEAD)
    for n in range(2):
        for k in range(4):
            b = n * 4 + k
            if is_self:
                here = slice(b * rows, (b + 1) * rows)
                rank[here, :] = jnp.broadcast_to(cols[:, 8 + b : 9 + b], (rows, 128))
                q, do = q_parts[b], do_parts[n][k, :rows, :]
                side = jnp.concatenate(
                    (do_parts[n][k, rows : rows + 16, :], do_parts[n][k, rows + 16 :, :]), axis=1
                )
            else:
                q, do = both_parts[n][k, :rows, :PAIR], both_parts[n][k, :rows, PAIR:]
                side = both_parts[n][k, rows:, :]
            side = side_lanes(side, core)
            q_all[b] = jnp.where(mine, (q * 0.125).astype(low_t), side)
            do_all[b] = jnp.where(mine, do, side)
    dk[...] = jnp.zeros_like(dk)
    dv[...] = jnp.zeros_like(dv)
    tile = min(1024, keys)
    blocks = 1 if is_self else 2

    def step(step, carry):
        b, wide = step * blocks, blocks * rows
        q, do = (ref[pl.ds(b, blocks)].reshape(wide, PAIR) for ref in (q_all, do_all))
        dqt = jnp.zeros((HEAD, wide), wide_t)
        for t in range(keys // tile):
            here = slice(t * tile, (t + 1) * tile)
            w = jnp.exp(dot_nt(k_all[here, :], q))
            if is_self:
                ranks = jnp.concatenate((rank[here, :],) * (wide // 128), axis=1)
                index = lax.broadcasted_iota(jnp.int32, (tile, wide), 0)
                own = lax.broadcasted_iota(jnp.int32, (tile, wide), 1) + (b * rows - t * tile)
                w = jnp.where((ranks < row_data[pl.ds(8 + b, 1), :]) | (index == own), w, 0.0)
            ds = (w * dot_nt(v_all[here, :], do)).astype(low_t)
            dv[here, :] += dot_nn(w.astype(low_t), do)
            dk[here, :] += dot_nn(ds, q)
            dqt = dqt + dot_nn(kt[:, here], ds)
        dqt = (dqt * 0.125).astype(low_t)
        for n in range(blocks):
            dq_t[b + n] = dqt[:, n * rows : (n + 1) * rows]
        return carry

    lax.fori_loop(0, 8 // blocks, step, 0)
    for n in range(2):
        for k in range(4):
            b = n * 4 + k
            device = k * 2 + (core ^ n)
            here = slice(b * rows, (b + 1) * rows)
            if is_self:
                back[device, :HEAD, :] = dq_t[b]
            else:
                (dq_keep, dq_send)[n][k] = dq_t[b]
            out, start = (back, HEAD) if is_self else (dkv, 0)
            for value in (dk, dv):
                turn[...] = value[here, :].T
                out[device, start : start + HEAD, :] = turn[features, :].astype(low_t)
                start += HEAD


def head_grads(grads, own, other, core, hidden=None):
    first = HEAD if hidden else 0
    total = jnp.zeros((2 * HEAD, D), wide_t)
    total_q = jnp.zeros((HEAD, D), wide_t)
    for n, part in enumerate((own, other)):
        for k in range(4):
            device = k * 2 + (core ^ n)
            total += dot_nn(grads[device, first:, :], part[k])
            if hidden:
                total_q += dot_nn(grads[device, :HEAD, :], hidden[n][k])
    return total, total_q


def pair_grads(ids, grads, own, other, dw):
    total, unused = head_grads(grads, own, other, ids[1])
    for w in range(4):
        dw[w] = total[:, w * 128 : (w + 1) * 128].astype(low_t)


def turned(value):
    return value.astype(wide_t).T.astype(low_t)


def pair_up(ids, keep, received, *outs):
    for k in range(4):
        p = ids[0] ^ k
        outs[k][at16(ids[1] * HEAD, HEAD), :] = keep[p]
        outs[k][at16((1 - ids[1]) * HEAD, HEAD), :] = received[p]


def first_back(ids, *refs):
    parts = refs[:4]
    second_grad, normed, scale, self_mixed, lse, row_data, gs, wcq, wo, sums_in = refs[4:14]
    first_grad, branch, dealt, dq, sums, all_t = refs[14:]
    for k in range(4):
        all_t[at128((ids[0] ^ k) * PAIR), :] = parts[k][...]
    dq[...] = turned(all_t[...])
    total = second_grad[...] + dot_nt(dq[...], wcq[...])
    grad, gain_a, shift_a = layer_norm_back(
        total, normed[...], scale[:, 0:1], gs[0:1, :].astype(wide_t)
    )
    first_grad[...] = grad
    low = grad.astype(low_t)
    branch[...] = low
    mixed = dot_nt(low, wo[...]).astype(low_t)
    rows = low.shape[0]
    sides = side_rows(lse, mixed, self_mixed, row_data)
    for p in range(PAIRS):
        dealt[p, :rows, :] = mixed[:, p * PAIR : (p + 1) * PAIR]
        dealt[p, rows : rows + 16, :] = sides[p][:, :PAIR]
        dealt[p, rows + 16 :, :] = sides[p][:, PAIR:]
    zero = jnp.zeros_like(gain_a)
    sums[...] = sums_in[...] + jnp.concatenate(
        (gain_a, zero, zero, shift_a, zero, zero, zero, zero), axis=0
    )


def source_back(ids, parts, wckv, out, dkv):
    rows = out.shape[0]
    for device in range(8):
        for n in range(2):
            start = 2 * D + 128 + n * rows
            dkv[n * D + device * HEAD : n * D + (device + 1) * HEAD, :] = parts[
                device, :, start : start + rows
            ]
    out[...] = dot_nt(turned(dkv[...]), wckv[...])


def hidden_back(ids, back, first_grad, wq, wkv, hidden_grad, stream_grad, all_t):
    for device in range(8):
        for n in range(3):
            all_t[n * D + device * HEAD : n * D + (device + 1) * HEAD, :] = back[
                device, n * HEAD : (n + 1) * HEAD, :
            ]
    hidden_grad[...] = first_grad[...] + dot_nt(turned(all_t[:D, :]), wq[...])
    stream_grad[...] = dot_nt(turned(all_t[D:, :]), wkv[...])


def add_parts(parts, rows, columns):
    total = parts[0, rows, columns].astype(wide_t)
    for n in range(1, parts.shape[0]):
        total = total + parts[n, rows, columns].astype(wide_t)
    return total.astype(low_t)


def add_chips(ids, parts, dw, *outs):
    width = parts.shape[2]
    for e in range(4):
        outs[e][:, :width] = add_parts(parts, slice(e * 32, (e + 1) * 32), slice(None))
        piece = dw[ids[2] ^ e]
        for g in range(4):
            outs[e][:, width + g * 128 : width + (g + 1) * 128] = piece[g * 32 : (g + 1) * 32, :]


def self_grads(ids, grads, own, other, hidden_own, hidden_other, dw):
    total, total_q = head_grads(grads, own, other, ids[1], (hidden_own, hidden_other))
    for w in range(4):
        columns = slice(w * 128, (w + 1) * 128)
        dw[w, :HEAD, :] = total_q[:, columns].astype(low_t)
        dw[w, HEAD:, :] = total[:, columns].astype(low_t)


def end_sums(ids, parts, dw, *outs):
    width = 2 * D + 128
    for e in range(4):
        outs[e][:, :width] = add_parts(parts, slice(e * 16, (e + 1) * 16), slice(0, width))
        outs[e][:, width : width + 128] = jnp.zeros((16, 128), low_t)
        piece = dw[ids[2] ^ e]
        for g in range(12):
            start = width + 128 + g * 128
            outs[e][:, start : start + 128] = piece[g * 16 : (g + 1) * 16, :]


def add_shards(ids, *refs):
    out = refs[8]

    def total(parts):
        value = parts[0][...].astype(wide_t)
        for part in parts[1:]:
            value = value + part[...].astype(wide_t)
        return value.astype(low_t)

    first, last = total(refs[:4]), total(refs[4:8])
    width, half = first.shape[1], last.shape[1] // 2
    out[:, :width] = first
    out[:16, width:] = last[:, :half]
    out[16:, width:] = last[:, half:]


def place_all(ids, *refs):
    parts, refs = refs[:8], refs[8:]
    g_in, g_out, g_cross, g_cross_pair, g_cross_query, g_output, gains, shifts, g_query, g_pair = refs[:10]
    pair_t, all_t = refs[10:]
    half = FF // 2
    start_cross = half + 2 * D
    start_pair = start_cross + D // 2
    start_end = start_pair + 4 * 128
    half_end = parts[0].shape[1] - start_end
    for n in range(2):
        core = ids[1] ^ n
        for step in range(4):
            chip, part = ids[0] ^ step, parts[n * 4 + step]
            rows = at16(chip * 32, 32)
            device = chip * 2 + core
            for k in range(4):
                g_in[rows, at128(k * 512 + core * 256, 256)] = part[
                    :, k * 256 : (k + 1) * 256
                ].astype(wide_t)
            for g in range(2):
                g_out[at16(core * 256 + chip * 64 + g * 32, 32), :] = part[
                    :, half + g * D : half + (g + 1) * D
                ].astype(wide_t)
            g_cross[rows, at128(core * 256, 256)] = part[:, start_cross:start_pair].astype(wide_t)
            for g in range(4):
                column = start_pair + g * 128
                row = (g // 2) * D + device * HEAD + (g % 2) * 32
                pair_t[at16(row, 32), :] = part[:, column : column + 128].astype(wide_t)

            def piece(column, width):
                row, at = (0, column) if column < half_end else (16, column - half_end)
                return part[row : row + 16, start_end + at : start_end + at + width].astype(wide_t)

            own_rows = at16(device * 16)
            for column in range(0, D, 128):
                g_cross_query[own_rows, column : column + 128] = piece(column, 128)
                g_output[own_rows, column : column + 128] = piece(D + column, 128)
            if n == 0 and step == 0:
                norms = piece(2 * D, 128)
                gains[...], shifts[...] = norms[0:3], norms[3:6]
            for g in range(12):
                row = (g // 4) * D + device * HEAD + (g % 4) * 16
                all_t[at16(row), :] = piece(2 * D + 256 + g * 128, 128)
    g_cross_pair[...] = pair_t[...].T
    g_query[...] = all_t[:D, :].T
    g_pair[...] = all_t[D:, :].T


def pack_rows(ids, stream, source, many):
    for k in range(4):
        many[k, :, :D] = stream[...]
        many[k, :, D:] = source[...]


def pack_start(ids, wq, wkv, ffn_in, ffn_out, pack):
    own = ids[0] * 2 + ids[1]
    for k in range(4):
        start = 3 * D + FF + k * D
        pack[:, start : start + D] = ffn_out[at16(own * 64 + k * 16), :]
    pack[:, :D] = wq[at16(own * 16), :]
    pack[:, D : 3 * D] = wkv[at16(own * 16), :]
    pack[:, 3 * D : 3 * D + FF] = ffn_in[at16(own * 16), :]


def pack_more(ids, *refs):
    weights, gain, shift, rows_in, pack, many = refs[:4], *refs[4:]
    rows = at16(ids[1] * 64, 64)
    norms = (gain[...].astype(wide_t), shift[...].astype(wide_t), jnp.zeros((58, 128), wide_t))
    norms = jnp.concatenate(norms, axis=0).astype(low_t)
    for k in range(4):
        start = 0
        for w in weights:
            pack[k, :, start : start + w.shape[1]] = w[rows, :]
            start += w.shape[1]
        pack[k, :, start:] = norms
        many[k] = rows_in[...]


def mask_data(ids, order, ranks, limits, cols, row_data, all_rows):
    rows = cols.shape[0]
    ends = [ids[3]]
    for n in range(1, 4):
        ends.append(ends[-1] + ids[3 + n])

    def sequence(position):
        return sum((position >= end).astype(wide_t) for end in ends)

    for n in range(2):
        for k in range(4):
            b = n * 4 + k
            device = k * 2 + (ids[1] ^ n)
            here = at128(device * rows, rows)
            index = lax.broadcasted_iota(jnp.int32, (1, rows), 1) + device * rows
            all_rows[b : b + 1, :] = sequence(order[:, here])
            all_rows[8 + b : 9 + b, :] = ranks[:, here].astype(wide_t)
            all_rows[16 + b : 17 + b, :] = sequence(index)
            row_data[8 + b : 9 + b, :] = limits[:, here].astype(wide_t)
    row_data[0:8, :] = all_rows[0:8, :]
    all_rows[24:32, :] = jnp.zeros((8, rows), wide_t)
    all_rows[24:25, :] = all_rows[pl.ds(ids[0], 1), :]
    row_data[16:24, :] = jnp.zeros((8, rows), wide_t)
    row_data[16:17, :] = all_rows[pl.ds(ids[0], 1), :]
    row_data[17:18, :] = row_data[pl.ds(8 + ids[0], 1), :]
    cols[:, :32] = all_rows[...].T


def pack_first(ids, *refs):
    parts, (one, two) = refs[:4], refs[4:]
    width = one.shape[1]
    for e in range(4):
        here = slice(e * 16, (e + 1) * 16)
        one[here, :] = parts[e][:, :width]
        two[here, :] = parts[e][:, width:]


def core_swap(value):
    return lax.ppermute(value, "core", [(0, 1), (1, 0)])


def chip_swaps(parts):
    moves = [[(i, i ^ k) for i in range(4)] for k in range(4)]
    return [parts[0]] + [lax.ppermute(parts[k], "chip", moves[k]) for k in range(1, 4)]


def shard_swaps(parts):
    moves = [[(i, i ^ k) for i in range(4)] for k in range(4)]
    return [parts[0]] + [lax.ppermute(parts[k], "wa", moves[k]) for k in range(1, 4)]


def deal(value):
    return lax.all_to_all(value, "chip", 0, 0, tiled=True)


def deal_all(value):
    return lax.all_to_all(value, ("chip", "core"), 0, 0, tiled=True)


def deal_both(value):
    own = deal(value)
    return own, core_swap(own)


def after(value, *others):
    return lax.optimization_barrier((value,) + others)[0]


def fast_shards(
    hidden,
    stream,
    encoder,
    lengths,
    order,
    ranks,
    thresholds,
    self_query,
    self_key_value,
    self_output,
    cross_query,
    cross_key_value,
    cross_output,
    ffn_in,
    ffn_out,
    norm_gain,
    norm_shift,
    cotangent,
):
    rows, keys = hidden.shape[1], order.shape[1]
    chip, core, mw = lax.axis_index("chip"), lax.axis_index("core"), lax.axis_index("wa")
    ids = jnp.stack((chip, core, mw)).astype(jnp.int32)
    inputs = hidden[0]

    (many,) = run(pack_rows, [((4, rows, 2 * D), low_t)], ids, [stream[0], encoder[0]])
    (pack1,) = run(
        pack_start,
        [((16, 3 * D + 2 * FF), low_t)],
        ids,
        [after(self_query, many), self_key_value, ffn_in, ffn_out],
    )
    x_own = deal(many)
    shards1 = shard_swaps([pack1] * 4)
    copies2, hidden_copies = run(
        pack_more,
        [((4, 64, 5 * D + 128), low_t), ((4, rows, D), low_t)],
        ids,
        [after(self_output, pack1), cross_query, cross_key_value, cross_output, norm_gain, norm_shift]
        + [inputs],
    )
    cols, row_data = run(
        mask_data,
        [((rows, 32), wide_t), ((24, rows), wide_t)],
        jnp.concatenate((after(ids, pack1), lengths[0])),
        [order, ranks, thresholds],
        [((32, rows), wide_t)],
    )
    part1, part3 = run(
        pack_first,
        [((64, 3 * D), low_t), ((64, 2 * FF), low_t)],
        ids,
        [after(shards1[0], x_own, cols, copies2)] + shards1[1:],
    )
    slices1 = chip_swaps([part1] * 4)
    slices1 = slices1 + [core_swap(part) for part in slices1]
    shards2 = lax.all_to_all(after(copies2, x_own), "wa", 0, 0, tiled=True)
    x_other = core_swap(after(x_own, part1))
    slices3 = chip_swaps([after(part3, slices1[1])] * 4)
    stream_own, stream_other = (x_own, 0), (x_other, 0)
    source_own, source_other = (x_own, 1), (x_other, 1)

    attend_scratch = [
        ((rows, D), low_t),
        ((keys, D), low_t),
        ((D, keys), low_t),
        ((D, D), low_t),
        ((keys, rows), wide_t),
        ((2, keys, rows), wide_t),
        ((D, rows), wide_t),
    ]
    self_low, self_mixed, self_lse, wq, wkv = run(
        self_forward,
        [((rows, D), low_t), ((rows, D), wide_t), ((HEADS, rows), wide_t)]
        + [((D, D), low_t), ((D, 2 * D), low_t)],
        ids,
        [inputs, stream_own, stream_other, *slices1, cols, row_data],
        attend_scratch,
        us=15,
    )
    head_shapes = [((keys, PAIR), low_t)] * 2 + [((HEAD, keys), low_t)]
    self_head = run(
        functools.partial(pair_setup, True),
        head_shapes,
        ids,
        [stream_own, stream_other, wkv, after(cols, self_low)],
        [((PAIR, rows), wide_t)],
        us=4,
    )
    slices3 = slices3 + [core_swap(after(part, self_head[0])) for part in slices3]
    shards2_other = core_swap(after(shards2, self_head[0], *slices3[:4]))
    hidden_own = deal(after(hidden_copies, shards2, self_head[0], *slices3[:4]))
    (
        first,
        normed,
        scale,
        first_low,
        cross_low,
        cross_mixed,
        cross_lse,
        cross_q,
        wo,
        wcq,
        wckv,
        wco,
        gs,
        *cross_head,
    ) = run(
        cross_forward,
        [((rows, D), wide_t)] * 2
        + [((rows, 128), wide_t)]
        + [((rows, D), low_t)] * 2
        + [((rows, D), wide_t), ((HEADS, rows), wide_t), ((rows, D), low_t)]
        + [((D, D), low_t), ((D, D), low_t), ((D, 2 * D), low_t), ((D, D), low_t), ((16, D), low_t)]
        + head_shapes,
        ids,
        [inputs, after(self_low, self_head[0]), source_own, source_other, shards2, shards2_other]
        + [cols, row_data],
        attend_scratch + [((PAIR, rows), wide_t)],
        us=15,
    )
    hidden_other = core_swap(after(hidden_own, cross_low))
    width_s = 2 * FF // 2 + 3 * D + D // 2
    result, cross_dealt, second_grad, keep_a, send_a, sums = run(
        feed_forward,
        [
            ((rows, D), low_t),
            ((PAIRS, rows + 16, 2 * PAIR), low_t),
            ((rows, D), wide_t),
            ((rows, width_s), low_t),
            ((rows, width_s), low_t),
            ((8, D), wide_t),
        ],
        ids,
        [after(first, hidden_own), cross_low, cross_mixed, cross_lse, row_data, cross_q, wco, gs]
        + [cotangent[0], *slices3],
        [((rows, FF), wide_t), ((2, D, FF // 2), low_t), ((2, FF // 2, D), low_t)],
        us=8,
    )
    both_own = deal(cross_dealt)
    width_a = FF // 2 + 2 * D + D // 2
    (dealt_a,) = run(
        grads_a,
        [((4, 128, width_a), low_t)],
        ids,
        [keep_a, core_swap(send_a)],
        [((D, FF // 2), low_t), ((FF // 2, D), low_t), ((D, D // 2), low_t)],
        us=6,
    )
    rows_a = deal(after(dealt_a, both_own))
    both_other = core_swap(after(both_own, dealt_a))

    back_scratch = (
        [((8, rows, PAIR), low_t)] * 2
        + [((8, HEAD, rows), low_t)]
        + [((keys, PAIR), wide_t)] * 3
        + [((PAIR, rows), wide_t)]
    )
    cq_keep, cq_send, cross_dkv = run(
        functools.partial(pair_back, False),
        [((4, HEAD, rows), low_t)] * 2 + [((8, 2 * HEAD, rows), low_t)],
        ids,
        [after(both_own, dealt_a), both_other, *cross_head],
        back_scratch,
        us=16,
    )
    pairs = run(pair_up, [((PAIR, rows), low_t)] * 4, ids, [cq_keep, core_swap(cq_send)])
    cross_back = chip_swaps(pairs)
    (self_queries,) = run(
        pair_queries,
        [((8, rows, PAIR), low_t)],
        ids,
        [hidden_own, hidden_other, after(wq, pairs[0])],
    )
    (cross_dw,) = run(
        pair_grads,
        [((4, 2 * HEAD, 128), low_t)],
        ids,
        [after(cross_dkv, pairs[0]), source_own, source_other],
    )
    first_grad, self_branch, self_dealt, cross_dq, sums = run(
        first_back,
        [
            ((rows, D), wide_t),
            ((rows, D), low_t),
            ((PAIRS, rows + 32, PAIR), low_t),
            ((rows, D), low_t),
            ((8, D), wide_t),
        ],
        ids,
        [after(cross_back[0], cross_dw, self_queries), *cross_back[1:], second_grad, normed, scale, self_mixed, self_lse, row_data, gs, wcq, wo, sums],
        [((D, rows), low_t)],
        us=4,
    )
    do_own = deal(after(self_dealt, rows_a))
    shards_a = run(
        add_chips,
        [((32, width_a + 512), low_t)] * 4,
        ids,
        [after(rows_a, first_grad), cross_dw],
    )
    moved_a = shard_swaps([after(part, do_own) for part in shards_a])
    (dealt_b,) = run(
        grads_b,
        [((8, 64, 2 * D + 128 + 2 * rows), low_t)],
        ids,
        [first_low, cross_dq, self_low, self_branch, sums, cross_dkv],
        [((D, D), low_t)] * 2,
        us=3,
    )
    rows_b = deal_all(after(dealt_b, do_own))
    do_other = core_swap(after(do_own, dealt_b, *shards_a))
    (self_back_t,) = run(
        functools.partial(pair_back, True),
        [((8, 3 * HEAD, rows), low_t)],
        ids,
        [self_queries, after(do_own, dealt_b, *shards_a), do_other, *self_head, cols, row_data],
        back_scratch,
        us=16,
    )
    end_width = 2 * D + 2 * 128 + 12 * 128
    (self_dw,) = run(
        self_grads,
        [((4, 3 * HEAD, 128), low_t)],
        ids,
        [self_back_t, stream_own, stream_other, hidden_own, hidden_other],
    )
    end_parts = run(
        end_sums, [((16, end_width), low_t)] * 4, ids, [after(rows_b, self_dw), self_dw]
    )
    moved_end = shard_swaps(end_parts)
    self_back = deal_all(after(self_back_t, end_parts[0], *moved_a))
    (source_grad,) = run(
        source_back,
        [((rows, D), wide_t)],
        ids,
        [rows_b, after(wckv, end_parts[0])],
        [((2 * D, rows), low_t)],
        us=3,
    )
    (sums_end,) = run(
        add_shards,
        [((32, width_a + 512 + end_width // 2), low_t)],
        ids,
        [*moved_a, after(moved_end[0], source_grad), *moved_end[1:]],
    )
    all_parts = chip_swaps([sums_end] * 4)
    hidden_grad, stream_grad = run(
        hidden_back,
        [((rows, D), wide_t)] * 2,
        ids,
        [self_back, first_grad, wq, wkv],
        [((3 * D, rows), low_t)],
        us=3,
    )
    all_parts = all_parts + [core_swap(after(part, hidden_grad)) for part in all_parts]
    (
        grad_in,
        grad_out,
        grad_cross_output,
        grad_cross_pair,
        grad_cross_query,
        grad_output,
        gain_grads,
        shift_grads,
        grad_query,
        grad_pair,
    ) = run(
        place_all,
        [((128, FF), wide_t), ((D, D), wide_t), ((128, D), wide_t), ((128, 2 * D), wide_t)]
        + [((128, D), wide_t)] * 2
        + [((3, 128), wide_t)] * 2
        + [((128, D), wide_t), ((128, 2 * D), wide_t)],
        ids,
        all_parts,
        [((2 * D, 128), wide_t), ((3 * D, 128), wide_t)],
    )
    return (
        result[None],
        hidden_grad[None],
        stream_grad[None],
        source_grad[None],
        grad_query,
        grad_pair,
        grad_output,
        grad_cross_query,
        grad_cross_pair,
        grad_cross_output,
        grad_in,
        grad_out,
        gain_grads,
        shift_grads,
    )


def solution(mesh):
    in_specs = (
        P("wa", "ctx", None),
        P("wa", "ctx", None),
        P("wa", "ctx", None),
        P("wa", None),
        P("wa", None),
        P("wa", None),
        P("wa", None),
        P("wa", None),
        P("wa", None),
        P("wa", None),
        P("wa", None),
        P("wa", None),
        P("wa", None),
        P("wa", None),
        P("wa", None),
        P(None, "wa"),
        P(None, "wa"),
        P("wa", "ctx", None),
    )
    out_specs = (
        P("wa", "ctx", None),
        P("wa", "ctx", None),
        P("wa", "ctx", None),
        P("wa", "ctx", None),
        P("wa", None),
        P("wa", None),
        P("wa", None),
        P("wa", None),
        P("wa", None),
        P("wa", None),
        P("wa", None),
        P("wa", None),
        P(None, "wa"),
        P(None, "wa"),
    )
    if mesh.axis_names != ("ctx", "wa") or mesh.shape["ctx"] != HEADS or mesh.shape["wa"] != 4:
        return jax.shard_map(
            general_shards, mesh=mesh, in_specs=in_specs, out_specs=out_specs, check_vma=False
        )

    def finer(spec):
        return P(*(("chip", "core") if axis == "ctx" else axis for axis in spec))

    return jax.shard_map(
        fast_shards,
        mesh=Mesh(mesh.devices.reshape(4, 2, 4), ("chip", "core", "wa")),
        in_specs=tuple(finer(spec) for spec in in_specs),
        out_specs=tuple(finer(spec) for spec in out_specs),
        check_vma=False,
    )
```

profile of v0, /device:TPU:0, one launch (start us, length us, event | category | flops | bytes accessed | tf_op | source)
XLA Modules:
  0.0 249.0 jit_solution(12102658242890990779)
XLA Ops:
  3.8 5.2 %all-to-all-start = ((bf16[4,256,1024]{2,1,0:T(8,128)(2,1)}), bf16[4,256,1024]{2,1,0:T(8,128)(2,1)S(1)}, u32[]{:S(2)}, u32[]{:S(2)}) async-start(bf16[4,256,1024]{2,1,0:T(8,128)(2,1)} %pack_rows.1), calls=%async_computation | async-start | bytes 4194304 | tf_op jit(solution)/shard_map/all_to_all | solution.py:1144
  11.0 3.7 %collective-permute-start.2 = (bf16[16,5632]{1,0:T(8,128)(2,1)}, bf16[16,5632]{1,0:T(8,128)(2,1)S(1)}, u32[]{:S(2)}, u32[]{:S(2)}) collective-permute-start(bf16[16,5632]{1,0:T(8,128)(2,1)} %pack_start.1.refs_0_), channel_id=1, source_target_pairs={{0,3},{1,2},{2,1},{3,0},{4,7},{5,6},{6,5},{7,4},{8,11},{9,10},{10,... | collective-permute-start | bytes 540680 | tf_op jit(solution)/shard_map/ppermute | solution.py:1140
  20.5 13.3 %all-to-all-done.refs_1_.refs_0_.refs_2_ = bf16[4,256,1024]{2,1,0:T(8,128)(2,1)S(1)} async-done(((bf16[4,256,1024]{2,1,0:T(8,128)(2,1)}), bf16[4,256,1024]{2,1,0:T(8,128)(2,1)S(1)}, u32[]{:S(2)}, u32[]{:S(2)}) %all-to-all-start) | async-done | bytes 2097184 | tf_op jit(solution)/shard_map/all_to_all | solution.py:1144
  41.1 5.0 %all-to-all-start.1 = ((bf16[4,64,2688]{2,1,0:T(8,128)(2,1)}), bf16[4,64,2688]{2,1,0:T(8,128)(2,1)S(1)}, u32[]{:S(2)}, u32[]{:S(2)}) async-start(bf16[4,64,2688]{2,1,0:T(8,128)(2,1)} %get-tuple-element.134), calls=%async_computation.1 | async-start | bytes 2752512 | tf_op jit(solution)/shard_map/all_to_all | solution.py:1216
  46.6 3.7 %collective-permute-done.5.refs_5_ = bf16[64,1536]{1,0:T(8,128)(2,1)} collective-permute-done((bf16[64,1536]{1,0:T(8,128)(2,1)}, bf16[64,1536]{1,0:T(8,128)(2,1)}, u32[]{:S(2)}, u32[]{:S(2)}) %collective-permute-start.5) | collective-permute-done | bytes 196640 | tf_op jit(solution)/shard_map/ppermute | solution.py:1135
  54.9 13.2 %self_forward.1 = (bf16[256,512]{1,0:T(8,128)(2,1)}, f32[256,512]{1,0:T(8,128)}, f32[8,256]{1,0:T(8,128)}, bf16[512,512]{1,0:T(8,128)(2,1)}, bf16[512,1024]{1,0:T(8,128)(2,1)}) custom-call(s32[3]{0:T(128)} %pad_add_fusion.ids, bf16[256,512]{1,0:T(8,128)(2,1)} %bitcast.15, bf16[4,256,1024]{2,1,0:T(8,128)(2,1)} %copy-done.1, ...), custom_call_target="tpu_custom_call" | custom-call | flops 15000000512 | bytes 8454144 | tf_op jit(solution)/shard_map/self_forward/pallas_call | solution.py:427
  68.2 5.1 %pair_setup.1 = (bf16[2048,128]{1,0:T(8,128)(2,1)}, bf16[2048,128]{1,0:T(8,128)(2,1)}, bf16[64,2048]{1,0:T(8,128)(2,1)}) custom-call(s32[3]{0:T(128)} %pad_add_fusion.ids, bf16[4,256,1024]{2,1,0:T(8,128)(2,1)} %copy-done.1, bf16[4,256,1024]{2,1,0:T(8,128)(2,1)} %collective-permute-done.3.refs_2_.refs_1_.refs_3_, ...), custom_call_target="tpu_custom_call" | custom-call | flops 4000000000 | bytes 6586368 | tf_op jit(solution)/shard_map/pair_setup/pallas_call | solution.py:427
  73.3 3.7 %collective-permute-done.12.refs_11_ = bf16[64,4096]{1,0:T(8,128)(2,1)S(1)} collective-permute-done((bf16[64,4096]{1,0:T(8,128)(2,1)}, bf16[64,4096]{1,0:T(8,128)(2,1)S(1)}, u32[]{:S(2)}, u32[]{:S(2)}) %collective-permute-start.12) | collective-permute-done | bytes 524320 | tf_op jit(solution)/shard_map/ppermute | solution.py:1135
  78.6 4.4 %all-to-all-start.2 = ((bf16[4,256,512]{2,1,0:T(8,128)(2,1)}), bf16[4,256,512]{2,1,0:T(8,128)(2,1)}, u32[]{:S(2)}, u32[]{:S(2)}) async-start(bf16[4,256,512]{2,1,0:T(8,128)(2,1)} %get-tuple-element.140), calls=%async_computation.2 | async-start | bytes 2097152 | tf_op jit(solution)/shard_map/all_to_all | solution.py:1144
  85.3 15.5 %cross_forward.1 = (f32[256,512]{1,0:T(8,128)}, f32[256,512]{1,0:T(8,128)}, f32[256,128]{1,0:T(8,128)}, bf16[256,512]{1,0:T(8,128)(2,1)}, bf16[256,512]{1,0:T(8,...) custom-call(s32[3]{0:T(128)} %pad_add_fusion.ids, ...), custom_call_target="tpu_custom_call" | custom-call | flops 15000000512 | bytes 13975552 | tf_op jit(solution)/shard_map/cross_forward/pallas_call | solution.py:427
  100.9 10.3 %feed_forward.1 = (bf16[256,512]{1,0:T(8,128)(2,1)}, bf16[4,272,256]{2,1,0:T(8,128)(2,1)}, f32[256,512]{1,0:T(8,128)}, bf16[256,3840]{1,0:T(8,128)(2,1)}, bf16[256,3840]{1,0:T(8,128)(2,1)}, /*index=5*/f32[8,512]{1,0:T(8,128)}) custom-call(s32[3]{0:T(128)} %pad_add_fusion.ids, f32[256,512]{1,0:T(8,128)} %get-tuple-element.141.refs_0_, ...), custom_call_target="tpu_custom_call" | custom-call | flops 8000000000 | bytes 11894784 | tf_op jit(solution)/shard_map/feed_forward/pallas_call | solution.py:427
  111.6 3.7 %all-to-all-start.3 = ((bf16[4,272,256]{2,1,0:T(8,128)(2,1)}), bf16[4,272,256]{2,1,0:T(8,128)(2,1)S(1)}, u32[]{:S(2)}, u32[]{:S(2)}) async-start(bf16[4,272,256]{2,1,0:T(8,128)(2,1)} %get-tuple-element.155), calls=%async_computation.3 | async-start | bytes 1114112 | tf_op jit(solution)/shard_map/all_to_all | solution.py:1144
  116.7 5.1 %grads_a.1 = bf16[4,128,2304]{2,1,0:T(8,128)(2,1)} custom-call(s32[3]{0:T(128)} %pad_add_fusion.ids, bf16[256,3840]{1,0:T(8,128)(2,1)} %get-tuple-element.156.refs_0_, bf16[256,3840]{1,0:T(8,128)(2,1)} %copy-done.8), custom_call_target="tpu_custom_call" | custom-call | flops 6000000000 | bytes 6291456 | tf_op jit(solution)/shard_map/grads_a/pallas_call | solution.py:427
  124.9 3.6 %all-to-all-start.4 = ((bf16[4,128,2304]{2,1,0:T(8,128)(2,1)}), bf16[4,128,2304]{2,1,0:T(8,128)(2,1)S(1)}, u32[]{:S(2)}, u32[]{:S(2)}) async-start(bf16[4,128,2304]{2,1,0:T(8,128)(2,1)} %grads_a.1), calls=%async_computation.4 | async-start | bytes 4718592 | tf_op jit(solution)/shard_map/all_to_all | solution.py:1144
  129.4 14.1 %pair_back.2 = (bf16[4,64,256]{2,1,0:T(8,128)(2,1)}, bf16[4,64,256]{2,1,0:T(8,128)(2,1)}, bf16[8,128,256]{2,1,0:T(8,128)(2,1)}) custom-call(s32[3]{0:T(128)} %pad_add_fusion.ids, bf16[4,272,256]{2,1,0:T(8,128)(2,1)} %copy-done.5, bf16[4,272,256]{2,1,0:T(8,128)(2,1)} %copy-done.10, bf16[2048,128]{1,0:T(8,128)(2,1)} %get-tuple-element.159.refs_2_, ...), custom_call_target="tpu_custom_call" | custom-call | flops 16000000000 | bytes 3211264 | tf_op jit(solution)/shard_map/pair_back/pallas_call | solution.py:427
  151.1 3.7 %pair_grads.1.refs_1_ = bf16[4,128,128]{2,1,0:T(8,128)(2,1)} custom-call(s32[3]{0:T(128)} %pad_add_fusion.ids, bf16[8,128,256]{2,1,0:T(8,128)(2,1)} %get-tuple-element.167.refs_0_.refs_5_, bf16[4,256,1024]{2,1,0:T(8,128)(2,1)} %copy-done.1, bf16[4,256,1024]{2,1,0:T(8,128)(2,1)} %collective-permute-done.3.refs_2_.refs_1_.refs_3_), custom_call_target="tpu_custom_call" | custom-call | flops 2000000000 | bytes 4849664 | tf_op jit(solution)/shard_map/pair_grads/pallas_call | solution.py:427
  160.7 3.7 %first_back.1 = (f32[256,512]{1,0:T(8,128)}, bf16[256,512]{1,0:T(8,128)(2,1)}, bf16[4,288,128]{2,1,0:T(8,128)(2,1)}, bf16[256,512]{1,0:T(8,128)(2,1)}, f32[8,512]{1,0:T(8,128)}) custom-call(s32[3]{0:T(128)} %pad_add_fusion.ids, bf16[128,256]{1,0:T(8,128)(2,1)} %get-tuple-element.168.refs_0_, bf16[128,256]{1,0:T(8,128)(2,1)} %copy-done.37, ...), custom_call_target="tpu_custom_call" | custom-call | flops 4000000000 | bytes 4440064 | tf_op jit(solution)/shard_map/first_back/pallas_call | solution.py:427
  178.2 4.2 %all-to-all-start.6 = ((bf16[8,64,1664]{2,1,0:T(8,128)(2,1)}), bf16[8,64,1664]{2,1,0:T(8,128)(2,1)S(1)}, u32[]{:S(2)}, u32[]{:S(2)}) async-start(bf16[8,64,1664]{2,1,0:T(8,128)(2,1)} %grads_b.1), calls=%async_computation.6 | async-start | bytes 3407872 | tf_op jit(solution)/shard_map/all_to_all | solution.py:1148
  183.1 18.1 %pair_back.3.refs_0_ = bf16[8,192,256]{2,1,0:T(8,128)(2,1)} custom-call(s32[3]{0:T(128)} %pad_add_fusion.ids, bf16[8,256,128]{2,1,0:T(8,128)(2,1)} %pair_queries.1.refs_0_, bf16[4,288,128]{2,1,0:T(8,128)(2,1)} %copy-done.6, bf16[4,288,128]{2,1,0:T(8,128)(2,1)} %copy-done.14, bf16[2048,128]{1,0:T(8,128)(2,1)} %get-tuple-element.132.refs_3_, ...), custom_call_target="tpu_custom_call" | custom-call | flops 16000000000 | bytes 3268608 | tf_op jit(solution)/shard_map/pair_back/pallas_call | solution.py:427
  201.2 4.8 %self_grads.1.refs_1_ = bf16[4,192,128]{2,1,0:T(8,128)(2,1)} custom-call(s32[3]{0:T(128)} %pad_add_fusion.ids, bf16[8,192,256]{2,1,0:T(8,128)(2,1)} %pair_back.3.refs_0_, bf16[4,256,1024]{2,1,0:T(8,128)(2,1)} %copy-done.1, bf16[4,256,1024]{2,1,0:T(8,128)(2,1)} %collective-permute-done.3.refs_2_.refs_1_.refs_3_, ...), custom_call_target="tpu_custom_call" | custom-call | flops 2000000000 | bytes 7274496 | tf_op jit(solution)/shard_map/self_grads/pallas_call | solution.py:427
  209.6 4.2 %all-to-all-start.7 = ((bf16[8,192,256]{2,1,0:T(8,128)(2,1)}), bf16[8,192,256]{2,1,0:T(8,128)(2,1)S(1)}, u32[]{:S(2)}, u32[]{:S(2)}) async-start(bf16[8,192,256]{2,1,0:T(8,128)(2,1)} %pair_back.3.refs_0_), calls=%async_computation.7 | async-start | bytes 1572864 | tf_op jit(solution)/shard_map/all_to_all | solution.py:1148
  214.1 3.5 %collective-permute-start.31 = (bf16[16,2816]{1,0:T(8,128)(2,1)}, bf16[16,2816]{1,0:T(8,128)(2,1)S(1)}, u32[]{:S(2)}, u32[]{:S(2)}) collective-permute-start(bf16[16,2816]{1,0:T(8,128)(2,1)} %get-tuple-element.210), channel_id=1, source_target_pairs={{0,2},{1,3},{2,0},{3,1},{4,6},{5,7},{6,4},{7,5},{8,10},{9,11},{10,... | collective-permute-start | bytes 270344 | tf_op jit(solution)/shard_map/ppermute | solution.py:1140
  221.3 3.8 %collective-permute-done.31.refs_6_ = bf16[16,2816]{1,0:T(8,128)(2,1)S(1)} collective-permute-done((bf16[16,2816]{1,0:T(8,128)(2,1)}, bf16[16,2816]{1,0:T(8,128)(2,1)S(1)}, u32[]{:S(2)}, u32[]{:S(2)}) %collective-permute-start.31) | collective-permute-done | bytes 90144 | tf_op jit(solution)/shard_map/ppermute | solution.py:1140
  244.9 3.9 %place_all.1 = (f32[128,2048]{1,0:T(8,128)}, f32[512,512]{1,0:T(8,128)}, f32[128,512]{1,0:T(8,128)}, f32[128,1024]{1,0:T(8,128)}, f32[128,512]{1,0:T(8,128)}, /*...) custom-call(s32[3]{0:T(128)} %pad_add_fusion.ids, ...), custom_call_target="tpu_custom_call" | custom-call | flops 2000000000 | bytes 6360064 | tf_op jit(solution)/shard_map/place_all/pallas_call | solution.py:427
  (180 shorter events, 88.0 us)
Async XLA Ops:
  3.8 30.0 %all-to-all-start = ((bf16[4,256,1024]{2,1,0:T(8,128)(2,1)}), bf16[4,256,1024]{2,1,0:T(8,128)(2,1)S(1)}, u32[]{:S(2)}, u32[]{:S(2)}) async-start(bf16[4,256,1024]{2,1,0:T(8,128)(2,1)} %pack_rows.1), calls=%async_computation | async-start | bytes 4194304 | tf_op jit(solution)/shard_map/all_to_all | solution.py:1144
  11.0 22.8 %collective-permute-start.2 = (bf16[16,5632]{1,0:T(8,128)(2,1)}, bf16[16,5632]{1,0:T(8,128)(2,1)S(1)}, u32[]{:S(2)}, u32[]{:S(2)}) collective-permute-start(bf16[16,5632]{1,0:T(8,128)(2,1)} %pack_start.1.refs_0_), channel_id=1, source_target_pairs={{0,3},{1,2},{2,1},{3,0},{4,7},{5,6},{6,5},{7,4},{8,11},{9,10},{10,... | collective-permute-start | bytes 540680 | tf_op jit(solution)/shard_map/ppermute | solution.py:1140
  14.7 19.1 %collective-permute-start.1 = (bf16[16,5632]{1,0:T(8,128)(2,1)}, bf16[16,5632]{1,0:T(8,128)(2,1)S(1)}, u32[]{:S(2)}, u32[]{:S(2)}) collective-permute-start(bf16[16,5632]{1,0:T(8,128)(2,1)} %pack_start.1.refs_0_), channel_id=1, source_target_pairs={{0,2},{1,3},{2,0},{3,1},{4,6},{5,7},{6,4},{7,5},{8,10},{9,11},{10,... | collective-permute-start | bytes 540680 | tf_op jit(solution)/shard_map/ppermute | solution.py:1140
  14.7 19.2 %collective-permute-start = (bf16[16,5632]{1,0:T(8,128)(2,1)}, bf16[16,5632]{1,0:T(8,128)(2,1)S(1)}, u32[]{:S(2)}, u32[]{:S(2)}) collective-permute-start(bf16[16,5632]{1,0:T(8,128)(2,1)} %pack_start.1.refs_0_), channel_id=1, source_target_pairs={{0,1},{1,0},{2,3},{3,2},{4,5},{5,4},{6,7},{7,6},{8,9},{9,8},{10,11... | collective-permute-start | bytes 540680 | tf_op jit(solution)/shard_map/ppermute | solution.py:1140
  37.4 16.9 %collective-permute-start.3 = (bf16[4,256,1024]{2,1,0:T(8,128)(2,1)S(1)}, bf16[4,256,1024]{2,1,0:T(8,128)(2,1)}, u32[]{:S(2)}, u32[]{:S(2)}) collective-permute-start(bf16[4,256,1024]{2,1,0:T(8,128)(2,1)S(1)} %all-to-all-done.refs_1_.refs_0_.refs_2_), channel_id=1, source_target_pairs={{0,4},{4,0},{1,5},{5,1},{2,6},{6,2},{3,7},{7,3},{8,12},{12,8},{9,1... | collective-permute-start | bytes 6291464 | tf_op jit(solution)/shard_map/ppermute | solution.py:1130
  39.0 11.3 %collective-permute-start.5 = (bf16[64,1536]{1,0:T(8,128)(2,1)}, bf16[64,1536]{1,0:T(8,128)(2,1)}, u32[]{:S(2)}, u32[]{:S(2)}) collective-permute-start(bf16[64,1536]{1,0:T(8,128)(2,1)} %get-tuple-element.126.refs_3_), channel_id=1, source_target_pairs={{0,16},{8,24},{16,0},{24,8},{1,17},{9,25},{17,1},{25,9},{2,18},{10... | collective-permute-start | bytes 589832 | tf_op jit(solution)/shard_map/ppermute | solution.py:1135
  41.1 37.5 %all-to-all-start.1 = ((bf16[4,64,2688]{2,1,0:T(8,128)(2,1)}), bf16[4,64,2688]{2,1,0:T(8,128)(2,1)S(1)}, u32[]{:S(2)}, u32[]{:S(2)}) async-start(bf16[4,64,2688]{2,1,0:T(8,128)(2,1)} %get-tuple-element.134), calls=%async_computation.1 | async-start | bytes 2752512 | tf_op jit(solution)/shard_map/all_to_all | solution.py:1216
  50.8 22.5 %collective-permute-start.13 = (bf16[64,4096]{1,0:T(8,128)(2,1)}, bf16[64,4096]{1,0:T(8,128)(2,1)S(1)}, u32[]{:S(2)}, u32[]{:S(2)}) collective-permute-start(bf16[64,4096]{1,0:T(8,128)(2,1)} %get-tuple-element.148.refs_9_), channel_id=1, source_target_pairs={{0,24},{8,16},{16,8},{24,0},{1,25},{9,17},{17,9},{25,1},{2,26},{10... | collective-permute-start | bytes 1572872 | tf_op jit(solution)/shard_map/ppermute | solution.py:1135
  52.2 24.8 %collective-permute-start.12 = (bf16[64,4096]{1,0:T(8,128)(2,1)}, bf16[64,4096]{1,0:T(8,128)(2,1)S(1)}, u32[]{:S(2)}, u32[]{:S(2)}) collective-permute-start(bf16[64,4096]{1,0:T(8,128)(2,1)} %get-tuple-element.148.refs_9_), channel_id=1, source_target_pairs={{0,16},{8,24},{16,0},{24,8},{1,17},{9,25},{17,1},{25,9},{2,18},{10... | collective-permute-start | bytes 1572872 | tf_op jit(solution)/shard_map/ppermute | solution.py:1135
  53.7 24.2 %collective-permute-start.11 = (bf16[64,4096]{1,0:T(8,128)(2,1)}, bf16[64,4096]{1,0:T(8,128)(2,1)}, u32[]{:S(2)}, u32[]{:S(2)}) collective-permute-start(bf16[64,4096]{1,0:T(8,128)(2,1)} %get-tuple-element.148.refs_9_), channel_id=1, source_target_pairs={{0,8},{8,0},{16,24},{24,16},{1,9},{9,1},{17,25},{25,17},{2,10},{10... | collective-permute-start | bytes 1572872 | tf_op jit(solution)/shard_map/ppermute | solution.py:1135
  78.6 22.2 %all-to-all-start.2 = ((bf16[4,256,512]{2,1,0:T(8,128)(2,1)}), bf16[4,256,512]{2,1,0:T(8,128)(2,1)}, u32[]{:S(2)}, u32[]{:S(2)}) async-start(bf16[4,256,512]{2,1,0:T(8,128)(2,1)} %get-tuple-element.140), calls=%async_computation.2 | async-start | bytes 2097152 | tf_op jit(solution)/shard_map/all_to_all | solution.py:1144
  83.0 17.8 %collective-permute-start.15 = (bf16[64,4096]{1,0:T(8,128)(2,1)S(1)}, bf16[64,4096]{1,0:T(8,128)(2,1)}, u32[]{:S(2)}, u32[]{:S(2)}) collective-permute-start(bf16[64,4096]{1,0:T(8,128)(2,1)S(1)} %copy-done.11), channel_id=1, source_target_pairs={{0,4},{4,0},{1,5},{5,1},{2,6},{6,2},{3,7},{7,3},{8,12},{12,8},{9,1... | collective-permute-start | bytes 1572872 | tf_op jit(solution)/shard_map/ppermute | solution.py:1130
  83.6 17.2 %collective-permute-start.16 = (bf16[64,4096]{1,0:T(8,128)(2,1)}, bf16[64,4096]{1,0:T(8,128)(2,1)}, u32[]{:S(2)}, u32[]{:S(2)}) collective-permute-start(bf16[64,4096]{1,0:T(8,128)(2,1)} %collective-permute-done.11.refs_10_), channel_id=1, source_target_pairs={{0,4},{4,0},{1,5},{5,1},{2,6},{6,2},{3,7},{7,3},{8,12},{12,8},{9,1... | collective-permute-start | bytes 1572872 | tf_op jit(solution)/shard_map/ppermute | solution.py:1130
  83.7 17.2 %collective-permute-start.17 = (bf16[64,4096]{1,0:T(8,128)(2,1)}, bf16[64,4096]{1,0:T(8,128)(2,1)}, u32[]{:S(2)}, u32[]{:S(2)}) collective-permute-start(bf16[64,4096]{1,0:T(8,128)(2,1)} %copy-done.13), channel_id=1, source_target_pairs={{0,4},{4,0},{1,5},{5,1},{2,6},{6,2},{3,7},{7,3},{8,12},{12,8},{9,1... | collective-permute-start | bytes 1572872 | tf_op jit(solution)/shard_map/ppermute | solution.py:1130
  84.1 16.7 %collective-permute-start.18 = (bf16[64,4096]{1,0:T(8,128)(2,1)}, bf16[64,4096]{1,0:T(8,128)(2,1)}, u32[]{:S(2)}, u32[]{:S(2)}) collective-permute-start(bf16[64,4096]{1,0:T(8,128)(2,1)} %copy-done.12), channel_id=1, source_target_pairs={{0,4},{4,0},{1,5},{5,1},{2,6},{6,2},{3,7},{7,3},{8,12},{12,8},{9,1... | collective-permute-start | bytes 1572872 | tf_op jit(solution)/shard_map/ppermute | solution.py:1130
  111.6 12.5 %all-to-all-start.3 = ((bf16[4,272,256]{2,1,0:T(8,128)(2,1)}), bf16[4,272,256]{2,1,0:T(8,128)(2,1)S(1)}, u32[]{:S(2)}, u32[]{:S(2)}) async-start(bf16[4,272,256]{2,1,0:T(8,128)(2,1)} %get-tuple-element.155), calls=%async_computation.3 | async-start | bytes 1114112 | tf_op jit(solution)/shard_map/all_to_all | solution.py:1144
  124.1 30.7 %collective-permute-start.19 = (bf16[4,256,512]{2,1,0:T(8,128)(2,1)}, bf16[4,256,512]{2,1,0:T(8,128)(2,1)}, u32[]{:S(2)}, u32[]{:S(2)}) collective-permute-start(bf16[4,256,512]{2,1,0:T(8,128)(2,1)} %all-to-all-done.2.refs_0_.refs_3_), channel_id=1, source_target_pairs={{0,4},{4,0},{1,5},{5,1},{2,6},{6,2},{3,7},{7,3},{8,12},{12,8},{9,1... | collective-permute-start | bytes 3145736 | tf_op jit(solution)/shard_map/ppermute | solution.py:1130
  124.9 39.5 %all-to-all-start.4 = ((bf16[4,128,2304]{2,1,0:T(8,128)(2,1)}), bf16[4,128,2304]{2,1,0:T(8,128)(2,1)S(1)}, u32[]{:S(2)}, u32[]{:S(2)}) async-start(bf16[4,128,2304]{2,1,0:T(8,128)(2,1)} %grads_a.1), calls=%async_computation.4 | async-start | bytes 4718592 | tf_op jit(solution)/shard_map/all_to_all | solution.py:1144
  173.8 35.8 %collective-permute-start.27 = (bf16[32,2816]{1,0:T(8,128)(2,1)}, bf16[32,2816]{1,0:T(8,128)(2,1)S(1)}, u32[]{:S(2)}, u32[]{:S(2)}) collective-permute-start(bf16[32,2816]{1,0:T(8,128)(2,1)} %get-tuple-element.200), channel_id=1, source_target_pairs={{0,1},{1,0},{2,3},{3,2},{4,5},{5,4},{6,7},{7,6},{8,9},{9,8},{10,11... | collective-permute-start | bytes 540680 | tf_op jit(solution)/shard_map/ppermute | solution.py:1140
  175.0 34.6 %collective-permute-start.28 = (bf16[32,2816]{1,0:T(8,128)(2,1)}, bf16[32,2816]{1,0:T(8,128)(2,1)S(1)}, u32[]{:S(2)}, u32[]{:S(2)}) collective-permute-start(bf16[32,2816]{1,0:T(8,128)(2,1)} %get-tuple-element.201), channel_id=1, source_target_pairs={{0,2},{1,3},{2,0},{3,1},{4,6},{5,7},{6,4},{7,5},{8,10},{9,11},{10,... | collective-permute-start | bytes 540680 | tf_op jit(solution)/shard_map/ppermute | solution.py:1140
  177.6 32.0 %collective-permute-start.29 = (bf16[32,2816]{1,0:T(8,128)(2,1)}, bf16[32,2816]{1,0:T(8,128)(2,1)S(1)}, u32[]{:S(2)}, u32[]{:S(2)}) collective-permute-start(bf16[32,2816]{1,0:T(8,128)(2,1)} %get-tuple-element.202), channel_id=1, source_target_pairs={{0,3},{1,2},{2,1},{3,0},{4,7},{5,6},{6,5},{7,4},{8,11},{9,10},{10,... | collective-permute-start | bytes 540680 | tf_op jit(solution)/shard_map/ppermute | solution.py:1140
  178.2 27.8 %all-to-all-start.6 = ((bf16[8,64,1664]{2,1,0:T(8,128)(2,1)}), bf16[8,64,1664]{2,1,0:T(8,128)(2,1)S(1)}, u32[]{:S(2)}, u32[]{:S(2)}) async-start(bf16[8,64,1664]{2,1,0:T(8,128)(2,1)} %grads_b.1), calls=%async_computation.6 | async-start | bytes 3407872 | tf_op jit(solution)/shard_map/all_to_all | solution.py:1148
  209.6 22.6 %all-to-all-start.7 = ((bf16[8,192,256]{2,1,0:T(8,128)(2,1)}), bf16[8,192,256]{2,1,0:T(8,128)(2,1)S(1)}, u32[]{:S(2)}, u32[]{:S(2)}) async-start(bf16[8,192,256]{2,1,0:T(8,128)(2,1)} %pair_back.3.refs_0_), calls=%async_computation.7 | async-start | bytes 1572864 | tf_op jit(solution)/shard_map/all_to_all | solution.py:1148
  214.1 11.0 %collective-permute-start.31 = (bf16[16,2816]{1,0:T(8,128)(2,1)}, bf16[16,2816]{1,0:T(8,128)(2,1)S(1)}, u32[]{:S(2)}, u32[]{:S(2)}) collective-permute-start(bf16[16,2816]{1,0:T(8,128)(2,1)} %get-tuple-element.210), channel_id=1, source_target_pairs={{0,2},{1,3},{2,0},{3,1},{4,6},{5,7},{6,4},{7,5},{8,10},{9,11},{10,... | collective-permute-start | bytes 270344 | tf_op jit(solution)/shard_map/ppermute | solution.py:1140
  (65 other events, 291.5 us)
where the time goes:
time: 251 us; the launch traced here: 249 us
  Pallas kernels  130 us (52%)
  starting transfers between devices  64.9 us (26%)
  waiting for transfers between devices  38.7 us (15%)
  local copies, waits for them, and re-layouts  12.8 us (5%)
    pallas_call x24, Pallas kernels, run(): pl.pallas_call(kernel, name=getattr(body, 'func', body).__name__, out_sha...  130 us
    all_to_all x5, starting transfers between devices, deal(): return lax.all_to_all(value, 'chip', 0, 0, tiled=True)  20.4 us
    all_to_all x5, waiting for transfers between devices, deal(): return lax.all_to_all(value, 'chip', 0, 0, tiled=True)  15.6 us
    ppermute x12, waiting for transfers between devices, chip_swaps(): lax.ppermute(parts[k], 'chip', moves[k])  15.5 us
    ppermute x12, starting transfers between devices, chip_swaps(): lax.ppermute(parts[k], 'chip', moves[k])  14.3 us
    ppermute x9, starting transfers between devices, shard_swaps(): lax.ppermute(parts[k], 'wa', moves[k])  13.3 us
    unnamed x82, local copies, waits for them, and re-layouts  12.8 us
    all_to_all x2, starting transfers between devices, deal_all(): return lax.all_to_all(value, ('chip', 'core'), 0, 0, tiled=True)  8.39 us
  transfers between devices with their start and end apart: 48, of which 15 were waited for; matrix products, arithmetic and copies ran while one was open for 0% of the time, Pallas kernels for 45%

commit v1 on v0

--- a/solution.py
+++ b/solution.py
@@ -841,7 +841,7 @@
             do_all[b] = jnp.where(mine, do, side)
     dk[...] = jnp.zeros_like(dk)
     dv[...] = jnp.zeros_like(dv)
-    tile = min(1024, keys)
+    tile = min(512 if is_self else 1024, keys)
     blocks = 1 if is_self else 2
 
     def step(step, carry):
@@ -850,12 +850,18 @@
         dqt = jnp.zeros((HEAD, wide), wide_t)
         for t in range(keys // tile):
             here = slice(t * tile, (t + 1) * tile)
+            if is_self:
+                start = (b * rows // tile + t) % (keys // tile) * tile
+                here = at128(start, tile)
             w = jnp.exp(dot_nt(k_all[here, :], q))
             if is_self:
                 ranks = jnp.concatenate((rank[here, :],) * (wide // 128), axis=1)
-                index = lax.broadcasted_iota(jnp.int32, (tile, wide), 0)
-                own = lax.broadcasted_iota(jnp.int32, (tile, wide), 1) + (b * rows - t * tile)
-                w = jnp.where((ranks < row_data[pl.ds(8 + b, 1), :]) | (index == own), w, 0.0)
+                seen = ranks < row_data[pl.ds(8 + b, 1), :]
+                if t == 0:
+                    index = lax.broadcasted_iota(jnp.int32, (tile, wide), 0)
+                    own = lax.broadcasted_iota(jnp.int32, (tile, wide), 1) + (b * rows - start)
+                    seen = seen | (index == own)
+                w = jnp.where(seen, w, 0.0)
             ds = (w * dot_nt(v_all[here, :], do)).astype(low_t)
             dv[here, :] += dot_nn(w.astype(low_t), do)
             dk[here, :] += dot_nn(ds, q)

time: 251 us -> 249 us (level)
  transfers between devices with their start and end apart: 48 -> 48, of which waited for: 15 -> 16; matrix products, arithmetic and copies ran while one was open for 0% -> 0% of each run, Pallas kernels for 45% -> 44%
where the time goes in v1:
time: 249 us; the launch traced here: 247 us
  Pallas kernels  128 us (51%)
  starting transfers between devices  64.2 us (26%)
  waiting for transfers between devices  39.3 us (16%)
  local copies, waits for them, and re-layouts  12.8 us (5%)
    pallas_call x24, Pallas kernels, run(): pl.pallas_call(kernel, name=getattr(body, 'func', body).__name__, out_sha...  128 us
    all_to_all x5, starting transfers between devices, deal(): return lax.all_to_all(value, 'chip', 0, 0, tiled=True)  20.4 us
    all_to_all x5, waiting for transfers between devices, deal(): return lax.all_to_all(value, 'chip', 0, 0, tiled=True)  15.6 us
    ppermute x12, waiting for transfers between devices, chip_swaps(): lax.ppermute(parts[k], 'chip', moves[k])  15.3 us
    ppermute x12, starting transfers between devices, chip_swaps(): lax.ppermute(parts[k], 'chip', moves[k])  14.2 us
    ppermute x9, starting transfers between devices, shard_swaps(): lax.ppermute(parts[k], 'wa', moves[k])  13.4 us
    unnamed x82, local copies, waits for them, and re-layouts  12.8 us
    all_to_all x2, starting transfers between devices, deal_all(): return lax.all_to_all(value, ('chip', 'core'), 0, 0, tiled=True)  7.72 us
  transfers between devices with their start and end apart: 48, of which 16 were waited for; matrix products, arithmetic and copies ran while one was open for 0% of the time, Pallas kernels for 44%

profile of v1, /device:TPU:0, one launch (start us, length us, event | category | flops | bytes accessed | tf_op | source)
XLA Modules:
  0.0 246.8 jit_solution(9222702524390459054)
XLA Ops:
  3.8 5.2 %all-to-all-start = ((bf16[4,256,1024]{2,1,0:T(8,128)(2,1)}), bf16[4,256,1024]{2,1,0:T(8,128)(2,1)S(1)}, u32[]{:S(2)}, u32[]{:S(2)}) async-start(bf16[4,256,1024]{2,1,0:T(8,128)(2,1)} %pack_rows.1), calls=%async_computation | async-start | bytes 4194304 | tf_op jit(solution)/shard_map/all_to_all | solution.py:1150
  11.0 3.7 %collective-permute-start.2 = (bf16[16,5632]{1,0:T(8,128)(2,1)}, bf16[16,5632]{1,0:T(8,128)(2,1)S(1)}, u32[]{:S(2)}, u32[]{:S(2)}) collective-permute-start(bf16[16,5632]{1,0:T(8,128)(2,1)} %pack_start.1.refs_0_), channel_id=1, source_target_pairs={{0,3},{1,2},{2,1},{3,0},{4,7},{5,6},{6,5},{7,4},{8,11},{9,10},{10,... | collective-permute-start | bytes 540680 | tf_op jit(solution)/shard_map/ppermute | solution.py:1146
  20.5 13.3 %all-to-all-done.refs_1_.refs_0_.refs_2_ = bf16[4,256,1024]{2,1,0:T(8,128)(2,1)S(1)} async-done(((bf16[4,256,1024]{2,1,0:T(8,128)(2,1)}), bf16[4,256,1024]{2,1,0:T(8,128)(2,1)S(1)}, u32[]{:S(2)}, u32[]{:S(2)}) %all-to-all-start) | async-done | bytes 2097184 | tf_op jit(solution)/shard_map/all_to_all | solution.py:1150
  41.1 5.0 %all-to-all-start.1 = ((bf16[4,64,2688]{2,1,0:T(8,128)(2,1)}), bf16[4,64,2688]{2,1,0:T(8,128)(2,1)S(1)}, u32[]{:S(2)}, u32[]{:S(2)}) async-start(bf16[4,64,2688]{2,1,0:T(8,128)(2,1)} %get-tuple-element.134), calls=%async_computation.1 | async-start | bytes 2752512 | tf_op jit(solution)/shard_map/all_to_all | solution.py:1222
  46.6 3.7 %collective-permute-done.5.refs_5_ = bf16[64,1536]{1,0:T(8,128)(2,1)} collective-permute-done((bf16[64,1536]{1,0:T(8,128)(2,1)}, bf16[64,1536]{1,0:T(8,128)(2,1)}, u32[]{:S(2)}, u32[]{:S(2)}) %collective-permute-start.5) | collective-permute-done | bytes 196640 | tf_op jit(solution)/shard_map/ppermute | solution.py:1141
  54.9 13.2 %self_forward.1 = (bf16[256,512]{1,0:T(8,128)(2,1)}, f32[256,512]{1,0:T(8,128)}, f32[8,256]{1,0:T(8,128)}, bf16[512,512]{1,0:T(8,128)(2,1)}, bf16[512,1024]{1,0:T(8,128)(2,1)}) custom-call(s32[3]{0:T(128)} %pad_add_fusion.ids, bf16[256,512]{1,0:T(8,128)(2,1)} %bitcast.15, bf16[4,256,1024]{2,1,0:T(8,128)(2,1)} %copy-done.1, ...), custom_call_target="tpu_custom_call" | custom-call | flops 15000000512 | bytes 8454144 | tf_op jit(solution)/shard_map/self_forward/pallas_call | solution.py:427
  68.2 5.1 %pair_setup.1 = (bf16[2048,128]{1,0:T(8,128)(2,1)}, bf16[2048,128]{1,0:T(8,128)(2,1)}, bf16[64,2048]{1,0:T(8,128)(2,1)}) custom-call(s32[3]{0:T(128)} %pad_add_fusion.ids, bf16[4,256,1024]{2,1,0:T(8,128)(2,1)} %copy-done.1, bf16[4,256,1024]{2,1,0:T(8,128)(2,1)} %collective-permute-done.3.refs_2_.refs_1_.refs_3_, ...), custom_call_target="tpu_custom_call" | custom-call | flops 4000000000 | bytes 6586368 | tf_op jit(solution)/shard_map/pair_setup/pallas_call | solution.py:427
  73.3 3.7 %collective-permute-done.12.refs_11_ = bf16[64,4096]{1,0:T(8,128)(2,1)S(1)} collective-permute-done((bf16[64,4096]{1,0:T(8,128)(2,1)}, bf16[64,4096]{1,0:T(8,128)(2,1)S(1)}, u32[]{:S(2)}, u32[]{:S(2)}) %collective-permute-start.12) | collective-permute-done | bytes 524320 | tf_op jit(solution)/shard_map/ppermute | solution.py:1141
  78.6 4.4 %all-to-all-start.2 = ((bf16[4,256,512]{2,1,0:T(8,128)(2,1)}), bf16[4,256,512]{2,1,0:T(8,128)(2,1)}, u32[]{:S(2)}, u32[]{:S(2)}) async-start(bf16[4,256,512]{2,1,0:T(8,128)(2,1)} %get-tuple-element.140), calls=%async_computation.2 | async-start | bytes 2097152 | tf_op jit(solution)/shard_map/all_to_all | solution.py:1150
  85.3 15.5 %cross_forward.1 = (f32[256,512]{1,0:T(8,128)}, f32[256,512]{1,0:T(8,128)}, f32[256,128]{1,0:T(8,128)}, bf16[256,512]{1,0:T(8,128)(2,1)}, bf16[256,512]{1,0:T(8,...) custom-call(s32[3]{0:T(128)} %pad_add_fusion.ids, ...), custom_call_target="tpu_custom_call" | custom-call | flops 15000000512 | bytes 13975552 | tf_op jit(solution)/shard_map/cross_forward/pallas_call | solution.py:427
  100.9 10.3 %feed_forward.1 = (bf16[256,512]{1,0:T(8,128)(2,1)}, bf16[4,272,256]{2,1,0:T(8,128)(2,1)}, f32[256,512]{1,0:T(8,128)}, bf16[256,3840]{1,0:T(8,128)(2,1)}, bf16[256,3840]{1,0:T(8,128)(2,1)}, /*index=5*/f32[8,512]{1,0:T(8,128)}) custom-call(s32[3]{0:T(128)} %pad_add_fusion.ids, f32[256,512]{1,0:T(8,128)} %get-tuple-element.141.refs_0_, ...), custom_call_target="tpu_custom_call" | custom-call | flops 8000000000 | bytes 11894784 | tf_op jit(solution)/shard_map/feed_forward/pallas_call | solution.py:427
  111.6 3.7 %all-to-all-start.3 = ((bf16[4,272,256]{2,1,0:T(8,128)(2,1)}), bf16[4,272,256]{2,1,0:T(8,128)(2,1)S(1)}, u32[]{:S(2)}, u32[]{:S(2)}) async-start(bf16[4,272,256]{2,1,0:T(8,128)(2,1)} %get-tuple-element.155), calls=%async_computation.3 | async-start | bytes 1114112 | tf_op jit(solution)/shard_map/all_to_all | solution.py:1150
  116.7 5.1 %grads_a.1 = bf16[4,128,2304]{2,1,0:T(8,128)(2,1)} custom-call(s32[3]{0:T(128)} %pad_add_fusion.ids, bf16[256,3840]{1,0:T(8,128)(2,1)} %get-tuple-element.156.refs_0_, bf16[256,3840]{1,0:T(8,128)(2,1)} %copy-done.8), custom_call_target="tpu_custom_call" | custom-call | flops 6000000000 | bytes 6291456 | tf_op jit(solution)/shard_map/grads_a/pallas_call | solution.py:427
  124.9 3.6 %all-to-all-start.4 = ((bf16[4,128,2304]{2,1,0:T(8,128)(2,1)}), bf16[4,128,2304]{2,1,0:T(8,128)(2,1)S(1)}, u32[]{:S(2)}, u32[]{:S(2)}) async-start(bf16[4,128,2304]{2,1,0:T(8,128)(2,1)} %grads_a.1), calls=%async_computation.4 | async-start | bytes 4718592 | tf_op jit(solution)/shard_map/all_to_all | solution.py:1150
  129.4 14.1 %pair_back.2 = (bf16[4,64,256]{2,1,0:T(8,128)(2,1)}, bf16[4,64,256]{2,1,0:T(8,128)(2,1)}, bf16[8,128,256]{2,1,0:T(8,128)(2,1)}) custom-call(s32[3]{0:T(128)} %pad_add_fusion.ids, bf16[4,272,256]{2,1,0:T(8,128)(2,1)} %copy-done.5, bf16[4,272,256]{2,1,0:T(8,128)(2,1)} %copy-done.10, bf16[2048,128]{1,0:T(8,128)(2,1)} %get-tuple-element.159.refs_2_, ...), custom_call_target="tpu_custom_call" | custom-call | flops 16000000000 | bytes 3211264 | tf_op jit(solution)/shard_map/pair_back/pallas_call | solution.py:427
  151.1 3.7 %pair_grads.1.refs_1_ = bf16[4,128,128]{2,1,0:T(8,128)(2,1)} custom-call(s32[3]{0:T(128)} %pad_add_fusion.ids, bf16[8,128,256]{2,1,0:T(8,128)(2,1)} %get-tuple-element.167.refs_0_.refs_5_, bf16[4,256,1024]{2,1,0:T(8,128)(2,1)} %copy-done.1, bf16[4,256,1024]{2,1,0:T(8,128)(2,1)} %collective-permute-done.3.refs_2_.refs_1_.refs_3_), custom_call_target="tpu_custom_call" | custom-call | flops 2000000000 | bytes 4849664 | tf_op jit(solution)/shard_map/pair_grads/pallas_call | solution.py:427
  160.7 3.7 %first_back.1 = (f32[256,512]{1,0:T(8,128)}, bf16[256,512]{1,0:T(8,128)(2,1)}, bf16[4,288,128]{2,1,0:T(8,128)(2,1)}, bf16[256,512]{1,0:T(8,128)(2,1)}, f32[8,512]{1,0:T(8,128)}) custom-call(s32[3]{0:T(128)} %pad_add_fusion.ids, bf16[128,256]{1,0:T(8,128)(2,1)} %get-tuple-element.168.refs_0_, bf16[128,256]{1,0:T(8,128)(2,1)} %copy-done.37, ...), custom_call_target="tpu_custom_call" | custom-call | flops 4000000000 | bytes 4440064 | tf_op jit(solution)/shard_map/first_back/pallas_call | solution.py:427
  164.4 3.5 %all-to-all-start.5 = ((bf16[4,288,128]{2,1,0:T(8,128)(2,1)}), bf16[4,288,128]{2,1,0:T(8,128)(2,1)S(1)}, u32[]{:S(2)}, u32[]{:S(2)}) async-start(bf16[4,288,128]{2,1,0:T(8,128)(2,1)} %get-tuple-element.182), calls=%async_computation.5 | async-start | bytes 589824 | tf_op jit(solution)/shard_map/all_to_all | solution.py:1150
  178.2 4.2 %all-to-all-start.6 = ((bf16[8,64,1664]{2,1,0:T(8,128)(2,1)}), bf16[8,64,1664]{2,1,0:T(8,128)(2,1)S(1)}, u32[]{:S(2)}, u32[]{:S(2)}) async-start(bf16[8,64,1664]{2,1,0:T(8,128)(2,1)} %grads_b.1), calls=%async_computation.6 | async-start | bytes 3407872 | tf_op jit(solution)/shard_map/all_to_all | solution.py:1154
  183.1 16.1 %pair_back.3.refs_0_ = bf16[8,192,256]{2,1,0:T(8,128)(2,1)} custom-call(s32[3]{0:T(128)} %pad_add_fusion.ids, bf16[8,256,128]{2,1,0:T(8,128)(2,1)} %pair_queries.1.refs_0_, bf16[4,288,128]{2,1,0:T(8,128)(2,1)} %copy-done.6, bf16[4,288,128]{2,1,0:T(8,128)(2,1)} %copy-done.14, bf16[2048,128]{1,0:T(8,128)(2,1)} %get-tuple-element.132.refs_3_, ...), custom_call_target="tpu_custom_call" | custom-call | flops 16000000000 | bytes 3268608 | tf_op jit(solution)/shard_map/pair_back/pallas_call | solution.py:427
  199.2 4.8 %self_grads.1.refs_1_ = bf16[4,192,128]{2,1,0:T(8,128)(2,1)} custom-call(s32[3]{0:T(128)} %pad_add_fusion.ids, bf16[8,192,256]{2,1,0:T(8,128)(2,1)} %pair_back.3.refs_0_, bf16[4,256,1024]{2,1,0:T(8,128)(2,1)} %copy-done.1, bf16[4,256,1024]{2,1,0:T(8,128)(2,1)} %collective-permute-done.3.refs_2_.refs_1_.refs_3_, ...), custom_call_target="tpu_custom_call" | custom-call | flops 2000000000 | bytes 7274496 | tf_op jit(solution)/shard_map/self_grads/pallas_call | solution.py:427
  208.3 3.6 %all-to-all-start.7 = ((bf16[8,192,256]{2,1,0:T(8,128)(2,1)}), bf16[8,192,256]{2,1,0:T(8,128)(2,1)S(1)}, u32[]{:S(2)}, u32[]{:S(2)}) async-start(bf16[8,192,256]{2,1,0:T(8,128)(2,1)} %pair_back.3.refs_0_), calls=%async_computation.7 | async-start | bytes 1572864 | tf_op jit(solution)/shard_map/all_to_all | solution.py:1154
  219.5 3.8 %collective-permute-done.31.refs_6_ = bf16[16,2816]{1,0:T(8,128)(2,1)S(1)} collective-permute-done((bf16[16,2816]{1,0:T(8,128)(2,1)}, bf16[16,2816]{1,0:T(8,128)(2,1)S(1)}, u32[]{:S(2)}, u32[]{:S(2)}) %collective-permute-start.31) | collective-permute-done | bytes 90144 | tf_op jit(solution)/shard_map/ppermute | solution.py:1146
  242.8 3.9 %place_all.1 = (f32[128,2048]{1,0:T(8,128)}, f32[512,512]{1,0:T(8,128)}, f32[128,512]{1,0:T(8,128)}, f32[128,1024]{1,0:T(8,128)}, f32[128,512]{1,0:T(8,128)}, /*...) custom-call(s32[3]{0:T(128)} %pad_add_fusion.ids, ...), custom_call_target="tpu_custom_call" | custom-call | flops 2000000000 | bytes 6360064 | tf_op jit(solution)/shard_map/place_all/pallas_call | solution.py:427
  (180 shorter events, 88.5 us)
Async XLA Ops:
  3.8 30.0 %all-to-all-start = ((bf16[4,256,1024]{2,1,0:T(8,128)(2,1)}), bf16[4,256,1024]{2,1,0:T(8,128)(2,1)S(1)}, u32[]{:S(2)}, u32[]{:S(2)}) async-start(bf16[4,256,1024]{2,1,0:T(8,128)(2,1)} %pack_rows.1), calls=%async_computation | async-start | bytes 4194304 | tf_op jit(solution)/shard_map/all_to_all | solution.py:1150
  11.0 22.8 %collective-permute-start.2 = (bf16[16,5632]{1,0:T(8,128)(2,1)}, bf16[16,5632]{1,0:T(8,128)(2,1)S(1)}, u32[]{:S(2)}, u32[]{:S(2)}) collective-permute-start(bf16[16,5632]{1,0:T(8,128)(2,1)} %pack_start.1.refs_0_), channel_id=1, source_target_pairs={{0,3},{1,2},{2,1},{3,0},{4,7},{5,6},{6,5},{7,4},{8,11},{9,10},{10,... | collective-permute-start | bytes 540680 | tf_op jit(solution)/shard_map/ppermute | solution.py:1146
  14.7 19.1 %collective-permute-start.1 = (bf16[16,5632]{1,0:T(8,128)(2,1)}, bf16[16,5632]{1,0:T(8,128)(2,1)S(1)}, u32[]{:S(2)}, u32[]{:S(2)}) collective-permute-start(bf16[16,5632]{1,0:T(8,128)(2,1)} %pack_start.1.refs_0_), channel_id=1, source_target_pairs={{0,2},{1,3},{2,0},{3,1},{4,6},{5,7},{6,4},{7,5},{8,10},{9,11},{10,... | collective-permute-start | bytes 540680 | tf_op jit(solution)/shard_map/ppermute | solution.py:1146
  14.7 19.2 %collective-permute-start = (bf16[16,5632]{1,0:T(8,128)(2,1)}, bf16[16,5632]{1,0:T(8,128)(2,1)S(1)}, u32[]{:S(2)}, u32[]{:S(2)}) collective-permute-start(bf16[16,5632]{1,0:T(8,128)(2,1)} %pack_start.1.refs_0_), channel_id=1, source_target_pairs={{0,1},{1,0},{2,3},{3,2},{4,5},{5,4},{6,7},{7,6},{8,9},{9,8},{10,11... | collective-permute-start | bytes 540680 | tf_op jit(solution)/shard_map/ppermute | solution.py:1146
  37.4 16.9 %collective-permute-start.3 = (bf16[4,256,1024]{2,1,0:T(8,128)(2,1)S(1)}, bf16[4,256,1024]{2,1,0:T(8,128)(2,1)}, u32[]{:S(2)}, u32[]{:S(2)}) collective-permute-start(bf16[4,256,1024]{2,1,0:T(8,128)(2,1)S(1)} %all-to-all-done.refs_1_.refs_0_.refs_2_), channel_id=1, source_target_pairs={{0,4},{4,0},{1,5},{5,1},{2,6},{6,2},{3,7},{7,3},{8,12},{12,8},{9,1... | collective-permute-start | bytes 6291464 | tf_op jit(solution)/shard_map/ppermute | solution.py:1136
  39.0 11.3 %collective-permute-start.5 = (bf16[64,1536]{1,0:T(8,128)(2,1)}, bf16[64,1536]{1,0:T(8,128)(2,1)}, u32[]{:S(2)}, u32[]{:S(2)}) collective-permute-start(bf16[64,1536]{1,0:T(8,128)(2,1)} %get-tuple-element.126.refs_3_), channel_id=1, source_target_pairs={{0,16},{8,24},{16,0},{24,8},{1,17},{9,25},{17,1},{25,9},{2,18},{10... | collective-permute-start | bytes 589832 | tf_op jit(solution)/shard_map/ppermute | solution.py:1141
  41.1 37.5 %all-to-all-start.1 = ((bf16[4,64,2688]{2,1,0:T(8,128)(2,1)}), bf16[4,64,2688]{2,1,0:T(8,128)(2,1)S(1)}, u32[]{:S(2)}, u32[]{:S(2)}) async-start(bf16[4,64,2688]{2,1,0:T(8,128)(2,1)} %get-tuple-element.134), calls=%async_computation.1 | async-start | bytes 2752512 | tf_op jit(solution)/shard_map/all_to_all | solution.py:1222
  50.8 22.5 %collective-permute-start.13 = (bf16[64,4096]{1,0:T(8,128)(2,1)}, bf16[64,4096]{1,0:T(8,128)(2,1)S(1)}, u32[]{:S(2)}, u32[]{:S(2)}) collective-permute-start(bf16[64,4096]{1,0:T(8,128)(2,1)} %get-tuple-element.148.refs_9_), channel_id=1, source_target_pairs={{0,24},{8,16},{16,8},{24,0},{1,25},{9,17},{17,9},{25,1},{2,26},{10... | collective-permute-start | bytes 1572872 | tf_op jit(solution)/shard_map/ppermute | solution.py:1141
  52.2 24.8 %collective-permute-start.12 = (bf16[64,4096]{1,0:T(8,128)(2,1)}, bf16[64,4096]{1,0:T(8,128)(2,1)S(1)}, u32[]{:S(2)}, u32[]{:S(2)}) collective-permute-start(bf16[64,4096]{1,0:T(8,128)(2,1)} %get-tuple-element.148.refs_9_), channel_id=1, source_target_pairs={{0,16},{8,24},{16,0},{24,8},{1,17},{9,25},{17,1},{25,9},{2,18},{10... | collective-permute-start | bytes 1572872 | tf_op jit(solution)/shard_map/ppermute | solution.py:1141
  53.7 24.2 %collective-permute-start.11 = (bf16[64,4096]{1,0:T(8,128)(2,1)}, bf16[64,4096]{1,0:T(8,128)(2,1)}, u32[]{:S(2)}, u32[]{:S(2)}) collective-permute-start(bf16[64,4096]{1,0:T(8,128)(2,1)} %get-tuple-element.148.refs_9_), channel_id=1, source_target_pairs={{0,8},{8,0},{16,24},{24,16},{1,9},{9,1},{17,25},{25,17},{2,10},{10... | collective-permute-start | bytes 1572872 | tf_op jit(solution)/shard_map/ppermute | solution.py:1141
  78.6 22.2 %all-to-all-start.2 = ((bf16[4,256,512]{2,1,0:T(8,128)(2,1)}), bf16[4,256,512]{2,1,0:T(8,128)(2,1)}, u32[]{:S(2)}, u32[]{:S(2)}) async-start(bf16[4,256,512]{2,1,0:T(8,128)(2,1)} %get-tuple-element.140), calls=%async_computation.2 | async-start | bytes 2097152 | tf_op jit(solution)/shard_map/all_to_all | solution.py:1150
  83.0 17.8 %collective-permute-start.15 = (bf16[64,4096]{1,0:T(8,128)(2,1)S(1)}, bf16[64,4096]{1,0:T(8,128)(2,1)}, u32[]{:S(2)}, u32[]{:S(2)}) collective-permute-start(bf16[64,4096]{1,0:T(8,128)(2,1)S(1)} %copy-done.11), channel_id=1, source_target_pairs={{0,4},{4,0},{1,5},{5,1},{2,6},{6,2},{3,7},{7,3},{8,12},{12,8},{9,1... | collective-permute-start | bytes 1572872 | tf_op jit(solution)/shard_map/ppermute | solution.py:1136
  83.6 17.2 %collective-permute-start.16 = (bf16[64,4096]{1,0:T(8,128)(2,1)}, bf16[64,4096]{1,0:T(8,128)(2,1)}, u32[]{:S(2)}, u32[]{:S(2)}) collective-permute-start(bf16[64,4096]{1,0:T(8,128)(2,1)} %collective-permute-done.11.refs_10_), channel_id=1, source_target_pairs={{0,4},{4,0},{1,5},{5,1},{2,6},{6,2},{3,7},{7,3},{8,12},{12,8},{9,1... | collective-permute-start | bytes 1572872 | tf_op jit(solution)/shard_map/ppermute | solution.py:1136
  83.7 17.2 %collective-permute-start.17 = (bf16[64,4096]{1,0:T(8,128)(2,1)}, bf16[64,4096]{1,0:T(8,128)(2,1)}, u32[]{:S(2)}, u32[]{:S(2)}) collective-permute-start(bf16[64,4096]{1,0:T(8,128)(2,1)} %copy-done.13), channel_id=1, source_target_pairs={{0,4},{4,0},{1,5},{5,1},{2,6},{6,2},{3,7},{7,3},{8,12},{12,8},{9,1... | collective-permute-start | bytes 1572872 | tf_op jit(solution)/shard_map/ppermute | solution.py:1136
  84.1 16.7 %collective-permute-start.18 = (bf16[64,4096]{1,0:T(8,128)(2,1)}, bf16[64,4096]{1,0:T(8,128)(2,1)}, u32[]{:S(2)}, u32[]{:S(2)}) collective-permute-start(bf16[64,4096]{1,0:T(8,128)(2,1)} %copy-done.12), channel_id=1, source_target_pairs={{0,4},{4,0},{1,5},{5,1},{2,6},{6,2},{3,7},{7,3},{8,12},{12,8},{9,1... | collective-permute-start | bytes 1572872 | tf_op jit(solution)/shard_map/ppermute | solution.py:1136
  111.6 12.5 %all-to-all-start.3 = ((bf16[4,272,256]{2,1,0:T(8,128)(2,1)}), bf16[4,272,256]{2,1,0:T(8,128)(2,1)S(1)}, u32[]{:S(2)}, u32[]{:S(2)}) async-start(bf16[4,272,256]{2,1,0:T(8,128)(2,1)} %get-tuple-element.155), calls=%async_computation.3 | async-start | bytes 1114112 | tf_op jit(solution)/shard_map/all_to_all | solution.py:1150
  124.1 30.7 %collective-permute-start.19 = (bf16[4,256,512]{2,1,0:T(8,128)(2,1)}, bf16[4,256,512]{2,1,0:T(8,128)(2,1)}, u32[]{:S(2)}, u32[]{:S(2)}) collective-permute-start(bf16[4,256,512]{2,1,0:T(8,128)(2,1)} %all-to-all-done.2.refs_0_.refs_3_), channel_id=1, source_target_pairs={{0,4},{4,0},{1,5},{5,1},{2,6},{6,2},{3,7},{7,3},{8,12},{12,8},{9,1... | collective-permute-start | bytes 3145736 | tf_op jit(solution)/shard_map/ppermute | solution.py:1136
  124.9 39.5 %all-to-all-start.4 = ((bf16[4,128,2304]{2,1,0:T(8,128)(2,1)}), bf16[4,128,2304]{2,1,0:T(8,128)(2,1)S(1)}, u32[]{:S(2)}, u32[]{:S(2)}) async-start(bf16[4,128,2304]{2,1,0:T(8,128)(2,1)} %grads_a.1), calls=%async_computation.4 | async-start | bytes 4718592 | tf_op jit(solution)/shard_map/all_to_all | solution.py:1150
  173.8 34.5 %collective-permute-start.27 = (bf16[32,2816]{1,0:T(8,128)(2,1)}, bf16[32,2816]{1,0:T(8,128)(2,1)S(1)}, u32[]{:S(2)}, u32[]{:S(2)}) collective-permute-start(bf16[32,2816]{1,0:T(8,128)(2,1)} %get-tuple-element.200), channel_id=1, source_target_pairs={{0,1},{1,0},{2,3},{3,2},{4,5},{5,4},{6,7},{7,6},{8,9},{9,8},{10,11... | collective-permute-start | bytes 540680 | tf_op jit(solution)/shard_map/ppermute | solution.py:1146
  175.0 33.3 %collective-permute-start.28 = (bf16[32,2816]{1,0:T(8,128)(2,1)}, bf16[32,2816]{1,0:T(8,128)(2,1)S(1)}, u32[]{:S(2)}, u32[]{:S(2)}) collective-permute-start(bf16[32,2816]{1,0:T(8,128)(2,1)} %get-tuple-element.201), channel_id=1, source_target_pairs={{0,2},{1,3},{2,0},{3,1},{4,6},{5,7},{6,4},{7,5},{8,10},{9,11},{10,... | collective-permute-start | bytes 540680 | tf_op jit(solution)/shard_map/ppermute | solution.py:1146
  177.6 30.8 %collective-permute-start.29 = (bf16[32,2816]{1,0:T(8,128)(2,1)}, bf16[32,2816]{1,0:T(8,128)(2,1)S(1)}, u32[]{:S(2)}, u32[]{:S(2)}) collective-permute-start(bf16[32,2816]{1,0:T(8,128)(2,1)} %get-tuple-element.202), channel_id=1, source_target_pairs={{0,3},{1,2},{2,1},{3,0},{4,7},{5,6},{6,5},{7,4},{8,11},{9,10},{10,... | collective-permute-start | bytes 540680 | tf_op jit(solution)/shard_map/ppermute | solution.py:1146
  178.2 26.6 %all-to-all-start.6 = ((bf16[8,64,1664]{2,1,0:T(8,128)(2,1)}), bf16[8,64,1664]{2,1,0:T(8,128)(2,1)S(1)}, u32[]{:S(2)}, u32[]{:S(2)}) async-start(bf16[8,64,1664]{2,1,0:T(8,128)(2,1)} %grads_b.1), calls=%async_computation.6 | async-start | bytes 3407872 | tf_op jit(solution)/shard_map/all_to_all | solution.py:1154
  208.3 22.0 %all-to-all-start.7 = ((bf16[8,192,256]{2,1,0:T(8,128)(2,1)}), bf16[8,192,256]{2,1,0:T(8,128)(2,1)S(1)}, u32[]{:S(2)}, u32[]{:S(2)}) async-start(bf16[8,192,256]{2,1,0:T(8,128)(2,1)} %pair_back.3.refs_0_), calls=%async_computation.7 | async-start | bytes 1572864 | tf_op jit(solution)/shard_map/all_to_all | solution.py:1154
  212.3 11.0 %collective-permute-start.31 = (bf16[16,2816]{1,0:T(8,128)(2,1)}, bf16[16,2816]{1,0:T(8,128)(2,1)S(1)}, u32[]{:S(2)}, u32[]{:S(2)}) collective-permute-start(bf16[16,2816]{1,0:T(8,128)(2,1)} %get-tuple-element.210), channel_id=1, source_target_pairs={{0,2},{1,3},{2,0},{3,1},{4,6},{5,7},{6,4},{7,5},{8,10},{9,11},{10,... | collective-permute-start | bytes 270344 | tf_op jit(solution)/shard_map/ppermute | solution.py:1146
  (65 other events, 288.7 us)

commit v2 on v1

--- a/solution.py
+++ b/solution.py
@@ -691,7 +691,7 @@
     for out in (keep, send):
         out[:, 2 * half_ff : 2 * half_ff + D] = low
         out[:, 2 * half_ff + 2 * D : 2 * half_ff + 3 * D] = cross_low[...]
-    width = 512
+    width = 1024
     chunks = [(n, c) for n in range(2) for c in range(FF // 2 // width)]
     total = second
     for n, c in chunks:

time: 249 us -> 248 us (level)
  no operation moved by 1% of the time
where the time goes in v2:
time: 248 us; the launch traced here: 246 us
  Pallas kernels  127 us (51%)
  starting transfers between devices  64.2 us (26%)
  waiting for transfers between devices  39.3 us (16%)
  local copies, waits for them, and re-layouts  12.8 us (5%)
    pallas_call x24, Pallas kernels, run(): pl.pallas_call(kernel, name=getattr(body, 'func', body).__name__, out_sha...  127 us
    all_to_all x5, starting transfers between devices, deal(): return lax.all_to_all(value, 'chip', 0, 0, tiled=True)  20.4 us
    all_to_all x5, waiting for transfers between devices, deal(): return lax.all_to_all(value, 'chip', 0, 0, tiled=True)  15.6 us
    ppermute x12, waiting for transfers between devices, chip_swaps(): lax.ppermute(parts[k], 'chip', moves[k])  15.3 us
    ppermute x12, starting transfers between devices, chip_swaps(): lax.ppermute(parts[k], 'chip', moves[k])  14.2 us
    ppermute x9, starting transfers between devices, shard_swaps(): lax.ppermute(parts[k], 'wa', moves[k])  13.4 us
    unnamed x82, local copies, waits for them, and re-layouts  12.8 us
    all_to_all x2, starting transfers between devices, deal_all(): return lax.all_to_all(value, ('chip', 'core'), 0, 0, tiled=True)  7.72 us
  transfers between devices with their start and end apart: 48, of which 16 were waited for; matrix products, arithmetic and copies ran while one was open for 0% of the time, Pallas kernels for 44%

profile of v2, /device:TPU:0, one launch (start us, length us, event | category | flops | bytes accessed | tf_op | source)
XLA Modules:
  0.0 246.1 jit_solution(2105199567347358355)
XLA Ops:
  3.8 5.2 %all-to-all-start = ((bf16[4,256,1024]{2,1,0:T(8,128)(2,1)}), bf16[4,256,1024]{2,1,0:T(8,128)(2,1)S(1)}, u32[]{:S(2)}, u32[]{:S(2)}) async-start(bf16[4,256,1024]{2,1,0:T(8,128)(2,1)} %pack_rows.1), calls=%async_computation | async-start | bytes 4194304 | tf_op jit(solution)/shard_map/all_to_all | solution.py:1150
  11.0 3.7 %collective-permute-start.2 = (bf16[16,5632]{1,0:T(8,128)(2,1)}, bf16[16,5632]{1,0:T(8,128)(2,1)S(1)}, u32[]{:S(2)}, u32[]{:S(2)}) collective-permute-start(bf16[16,5632]{1,0:T(8,128)(2,1)} %pack_start.1.refs_0_), channel_id=1, source_target_pairs={{0,3},{1,2},{2,1},{3,0},{4,7},{5,6},{6,5},{7,4},{8,11},{9,10},{10,... | collective-permute-start | bytes 540680 | tf_op jit(solution)/shard_map/ppermute | solution.py:1146
  20.5 13.3 %all-to-all-done.refs_1_.refs_0_.refs_2_ = bf16[4,256,1024]{2,1,0:T(8,128)(2,1)S(1)} async-done(((bf16[4,256,1024]{2,1,0:T(8,128)(2,1)}), bf16[4,256,1024]{2,1,0:T(8,128)(2,1)S(1)}, u32[]{:S(2)}, u32[]{:S(2)}) %all-to-all-start) | async-done | bytes 2097184 | tf_op jit(solution)/shard_map/all_to_all | solution.py:1150
  41.1 5.0 %all-to-all-start.1 = ((bf16[4,64,2688]{2,1,0:T(8,128)(2,1)}), bf16[4,64,2688]{2,1,0:T(8,128)(2,1)S(1)}, u32[]{:S(2)}, u32[]{:S(2)}) async-start(bf16[4,64,2688]{2,1,0:T(8,128)(2,1)} %get-tuple-element.134), calls=%async_computation.1 | async-start | bytes 2752512 | tf_op jit(solution)/shard_map/all_to_all | solution.py:1222
  46.6 3.7 %collective-permute-done.5.refs_5_ = bf16[64,1536]{1,0:T(8,128)(2,1)} collective-permute-done((bf16[64,1536]{1,0:T(8,128)(2,1)}, bf16[64,1536]{1,0:T(8,128)(2,1)}, u32[]{:S(2)}, u32[]{:S(2)}) %collective-permute-start.5) | collective-permute-done | bytes 196640 | tf_op jit(solution)/shard_map/ppermute | solution.py:1141
  54.9 13.2 %self_forward.1 = (bf16[256,512]{1,0:T(8,128)(2,1)}, f32[256,512]{1,0:T(8,128)}, f32[8,256]{1,0:T(8,128)}, bf16[512,512]{1,0:T(8,128)(2,1)}, bf16[512,1024]{1,0:T(8,128)(2,1)}) custom-call(s32[3]{0:T(128)} %pad_add_fusion.ids, bf16[256,512]{1,0:T(8,128)(2,1)} %bitcast.15, bf16[4,256,1024]{2,1,0:T(8,128)(2,1)} %copy-done.1, ...), custom_call_target="tpu_custom_call" | custom-call | flops 15000000512 | bytes 8454144 | tf_op jit(solution)/shard_map/self_forward/pallas_call | solution.py:427
  68.2 5.1 %pair_setup.1 = (bf16[2048,128]{1,0:T(8,128)(2,1)}, bf16[2048,128]{1,0:T(8,128)(2,1)}, bf16[64,2048]{1,0:T(8,128)(2,1)}) custom-call(s32[3]{0:T(128)} %pad_add_fusion.ids, bf16[4,256,1024]{2,1,0:T(8,128)(2,1)} %copy-done.1, bf16[4,256,1024]{2,1,0:T(8,128)(2,1)} %collective-permute-done.3.refs_2_.refs_1_.refs_3_, ...), custom_call_target="tpu_custom_call" | custom-call | flops 4000000000 | bytes 6586368 | tf_op jit(solution)/shard_map/pair_setup/pallas_call | solution.py:427
  73.3 3.7 %collective-permute-done.12.refs_11_ = bf16[64,4096]{1,0:T(8,128)(2,1)S(1)} collective-permute-done((bf16[64,4096]{1,0:T(8,128)(2,1)}, bf16[64,4096]{1,0:T(8,128)(2,1)S(1)}, u32[]{:S(2)}, u32[]{:S(2)}) %collective-permute-start.12) | collective-permute-done | bytes 524320 | tf_op jit(solution)/shard_map/ppermute | solution.py:1141
  78.6 4.4 %all-to-all-start.2 = ((bf16[4,256,512]{2,1,0:T(8,128)(2,1)}), bf16[4,256,512]{2,1,0:T(8,128)(2,1)}, u32[]{:S(2)}, u32[]{:S(2)}) async-start(bf16[4,256,512]{2,1,0:T(8,128)(2,1)} %get-tuple-element.140), calls=%async_computation.2 | async-start | bytes 2097152 | tf_op jit(solution)/shard_map/all_to_all | solution.py:1150
  85.3 15.5 %cross_forward.1 = (f32[256,512]{1,0:T(8,128)}, f32[256,512]{1,0:T(8,128)}, f32[256,128]{1,0:T(8,128)}, bf16[256,512]{1,0:T(8,128)(2,1)}, bf16[256,512]{1,0:T(8,...) custom-call(s32[3]{0:T(128)} %pad_add_fusion.ids, ...), custom_call_target="tpu_custom_call" | custom-call | flops 15000000512 | bytes 13975552 | tf_op jit(solution)/shard_map/cross_forward/pallas_call | solution.py:427
  100.9 9.5 %feed_forward.1 = (bf16[256,512]{1,0:T(8,128)(2,1)}, bf16[4,272,256]{2,1,0:T(8,128)(2,1)}, f32[256,512]{1,0:T(8,128)}, bf16[256,3840]{1,0:T(8,128)(2,1)}, bf16[256,3840]{1,0:T(8,128)(2,1)}, /*index=5*/f32[8,512]{1,0:T(8,128)}) custom-call(s32[3]{0:T(128)} %pad_add_fusion.ids, f32[256,512]{1,0:T(8,128)} %get-tuple-element.141.refs_0_, ...), custom_call_target="tpu_custom_call" | custom-call | flops 8000000000 | bytes 11894784 | tf_op jit(solution)/shard_map/feed_forward/pallas_call | solution.py:427
  110.9 3.7 %all-to-all-start.3 = ((bf16[4,272,256]{2,1,0:T(8,128)(2,1)}), bf16[4,272,256]{2,1,0:T(8,128)(2,1)S(1)}, u32[]{:S(2)}, u32[]{:S(2)}) async-start(bf16[4,272,256]{2,1,0:T(8,128)(2,1)} %get-tuple-element.155), calls=%async_computation.3 | async-start | bytes 1114112 | tf_op jit(solution)/shard_map/all_to_all | solution.py:1150
  116.0 5.1 %grads_a.1 = bf16[4,128,2304]{2,1,0:T(8,128)(2,1)} custom-call(s32[3]{0:T(128)} %pad_add_fusion.ids, bf16[256,3840]{1,0:T(8,128)(2,1)} %get-tuple-element.156.refs_0_, bf16[256,3840]{1,0:T(8,128)(2,1)} %copy-done.8), custom_call_target="tpu_custom_call" | custom-call | flops 6000000000 | bytes 6291456 | tf_op jit(solution)/shard_map/grads_a/pallas_call | solution.py:427
  124.1 3.6 %all-to-all-start.4 = ((bf16[4,128,2304]{2,1,0:T(8,128)(2,1)}), bf16[4,128,2304]{2,1,0:T(8,128)(2,1)S(1)}, u32[]{:S(2)}, u32[]{:S(2)}) async-start(bf16[4,128,2304]{2,1,0:T(8,128)(2,1)} %grads_a.1), calls=%async_computation.4 | async-start | bytes 4718592 | tf_op jit(solution)/shard_map/all_to_all | solution.py:1150
  128.6 14.1 %pair_back.2 = (bf16[4,64,256]{2,1,0:T(8,128)(2,1)}, bf16[4,64,256]{2,1,0:T(8,128)(2,1)}, bf16[8,128,256]{2,1,0:T(8,128)(2,1)}) custom-call(s32[3]{0:T(128)} %pad_add_fusion.ids, bf16[4,272,256]{2,1,0:T(8,128)(2,1)} %copy-done.5, bf16[4,272,256]{2,1,0:T(8,128)(2,1)} %copy-done.10, bf16[2048,128]{1,0:T(8,128)(2,1)} %get-tuple-element.159.refs_2_, ...), custom_call_target="tpu_custom_call" | custom-call | flops 16000000000 | bytes 3211264 | tf_op jit(solution)/shard_map/pair_back/pallas_call | solution.py:427
  150.3 3.7 %pair_grads.1.refs_1_ = bf16[4,128,128]{2,1,0:T(8,128)(2,1)} custom-call(s32[3]{0:T(128)} %pad_add_fusion.ids, bf16[8,128,256]{2,1,0:T(8,128)(2,1)} %get-tuple-element.167.refs_0_.refs_5_, bf16[4,256,1024]{2,1,0:T(8,128)(2,1)} %copy-done.1, bf16[4,256,1024]{2,1,0:T(8,128)(2,1)} %collective-permute-done.3.refs_2_.refs_1_.refs_3_), custom_call_target="tpu_custom_call" | custom-call | flops 2000000000 | bytes 4849664 | tf_op jit(solution)/shard_map/pair_grads/pallas_call | solution.py:427
  159.9 3.7 %first_back.1 = (f32[256,512]{1,0:T(8,128)}, bf16[256,512]{1,0:T(8,128)(2,1)}, bf16[4,288,128]{2,1,0:T(8,128)(2,1)}, bf16[256,512]{1,0:T(8,128)(2,1)}, f32[8,512]{1,0:T(8,128)}) custom-call(s32[3]{0:T(128)} %pad_add_fusion.ids, bf16[128,256]{1,0:T(8,128)(2,1)} %get-tuple-element.168.refs_0_, bf16[128,256]{1,0:T(8,128)(2,1)} %copy-done.37, ...), custom_call_target="tpu_custom_call" | custom-call | flops 4000000000 | bytes 4440064 | tf_op jit(solution)/shard_map/first_back/pallas_call | solution.py:427
  177.4 4.2 %all-to-all-start.6 = ((bf16[8,64,1664]{2,1,0:T(8,128)(2,1)}), bf16[8,64,1664]{2,1,0:T(8,128)(2,1)S(1)}, u32[]{:S(2)}, u32[]{:S(2)}) async-start(bf16[8,64,1664]{2,1,0:T(8,128)(2,1)} %grads_b.1), calls=%async_computation.6 | async-start | bytes 3407872 | tf_op jit(solution)/shard_map/all_to_all | solution.py:1154
  182.3 16.1 %pair_back.3.refs_0_ = bf16[8,192,256]{2,1,0:T(8,128)(2,1)} custom-call(s32[3]{0:T(128)} %pad_add_fusion.ids, bf16[8,256,128]{2,1,0:T(8,128)(2,1)} %pair_queries.1.refs_0_, bf16[4,288,128]{2,1,0:T(8,128)(2,1)} %copy-done.6, bf16[4,288,128]{2,1,0:T(8,128)(2,1)} %copy-done.14, bf16[2048,128]{1,0:T(8,128)(2,1)} %get-tuple-element.132.refs_3_, ...), custom_call_target="tpu_custom_call" | custom-call | flops 16000000000 | bytes 3268608 | tf_op jit(solution)/shard_map/pair_back/pallas_call | solution.py:427
  198.5 4.8 %self_grads.1.refs_1_ = bf16[4,192,128]{2,1,0:T(8,128)(2,1)} custom-call(s32[3]{0:T(128)} %pad_add_fusion.ids, bf16[8,192,256]{2,1,0:T(8,128)(2,1)} %pair_back.3.refs_0_, bf16[4,256,1024]{2,1,0:T(8,128)(2,1)} %copy-done.1, bf16[4,256,1024]{2,1,0:T(8,128)(2,1)} %collective-permute-done.3.refs_2_.refs_1_.refs_3_, ...), custom_call_target="tpu_custom_call" | custom-call | flops 2000000000 | bytes 7274496 | tf_op jit(solution)/shard_map/self_grads/pallas_call | solution.py:427
  207.6 3.6 %all-to-all-start.7 = ((bf16[8,192,256]{2,1,0:T(8,128)(2,1)}), bf16[8,192,256]{2,1,0:T(8,128)(2,1)S(1)}, u32[]{:S(2)}, u32[]{:S(2)}) async-start(bf16[8,192,256]{2,1,0:T(8,128)(2,1)} %pair_back.3.refs_0_), calls=%async_computation.7 | async-start | bytes 1572864 | tf_op jit(solution)/shard_map/all_to_all | solution.py:1154
  211.5 3.5 %collective-permute-start.31 = (bf16[16,2816]{1,0:T(8,128)(2,1)}, bf16[16,2816]{1,0:T(8,128)(2,1)S(1)}, u32[]{:S(2)}, u32[]{:S(2)}) collective-permute-start(bf16[16,2816]{1,0:T(8,128)(2,1)} %get-tuple-element.210), channel_id=1, source_target_pairs={{0,2},{1,3},{2,0},{3,1},{4,6},{5,7},{6,4},{7,5},{8,10},{9,11},{10,... | collective-permute-start | bytes 270344 | tf_op jit(solution)/shard_map/ppermute | solution.py:1146
  218.7 3.8 %collective-permute-done.31.refs_6_ = bf16[16,2816]{1,0:T(8,128)(2,1)S(1)} collective-permute-done((bf16[16,2816]{1,0:T(8,128)(2,1)}, bf16[16,2816]{1,0:T(8,128)(2,1)S(1)}, u32[]{:S(2)}, u32[]{:S(2)}) %collective-permute-start.31) | collective-permute-done | bytes 90144 | tf_op jit(solution)/shard_map/ppermute | solution.py:1146
  242.0 3.9 %place_all.1 = (f32[128,2048]{1,0:T(8,128)}, f32[512,512]{1,0:T(8,128)}, f32[128,512]{1,0:T(8,128)}, f32[128,1024]{1,0:T(8,128)}, f32[128,512]{1,0:T(8,128)}, /*...) custom-call(s32[3]{0:T(128)} %pad_add_fusion.ids, ...), custom_call_target="tpu_custom_call" | custom-call | flops 2000000000 | bytes 6360064 | tf_op jit(solution)/shard_map/place_all/pallas_call | solution.py:427
  (180 shorter events, 88.5 us)
Async XLA Ops:
  3.8 30.0 %all-to-all-start = ((bf16[4,256,1024]{2,1,0:T(8,128)(2,1)}), bf16[4,256,1024]{2,1,0:T(8,128)(2,1)S(1)}, u32[]{:S(2)}, u32[]{:S(2)}) async-start(bf16[4,256,1024]{2,1,0:T(8,128)(2,1)} %pack_rows.1), calls=%async_computation | async-start | bytes 4194304 | tf_op jit(solution)/shard_map/all_to_all | solution.py:1150
  11.0 22.8 %collective-permute-start.2 = (bf16[16,5632]{1,0:T(8,128)(2,1)}, bf16[16,5632]{1,0:T(8,128)(2,1)S(1)}, u32[]{:S(2)}, u32[]{:S(2)}) collective-permute-start(bf16[16,5632]{1,0:T(8,128)(2,1)} %pack_start.1.refs_0_), channel_id=1, source_target_pairs={{0,3},{1,2},{2,1},{3,0},{4,7},{5,6},{6,5},{7,4},{8,11},{9,10},{10,... | collective-permute-start | bytes 540680 | tf_op jit(solution)/shard_map/ppermute | solution.py:1146
  14.7 19.1 %collective-permute-start.1 = (bf16[16,5632]{1,0:T(8,128)(2,1)}, bf16[16,5632]{1,0:T(8,128)(2,1)S(1)}, u32[]{:S(2)}, u32[]{:S(2)}) collective-permute-start(bf16[16,5632]{1,0:T(8,128)(2,1)} %pack_start.1.refs_0_), channel_id=1, source_target_pairs={{0,2},{1,3},{2,0},{3,1},{4,6},{5,7},{6,4},{7,5},{8,10},{9,11},{10,... | collective-permute-start | bytes 540680 | tf_op jit(solution)/shard_map/ppermute | solution.py:1146
  14.7 19.2 %collective-permute-start = (bf16[16,5632]{1,0:T(8,128)(2,1)}, bf16[16,5632]{1,0:T(8,128)(2,1)S(1)}, u32[]{:S(2)}, u32[]{:S(2)}) collective-permute-start(bf16[16,5632]{1,0:T(8,128)(2,1)} %pack_start.1.refs_0_), channel_id=1, source_target_pairs={{0,1},{1,0},{2,3},{3,2},{4,5},{5,4},{6,7},{7,6},{8,9},{9,8},{10,11... | collective-permute-start | bytes 540680 | tf_op jit(solution)/shard_map/ppermute | solution.py:1146
  37.4 16.9 %collective-permute-start.3 = (bf16[4,256,1024]{2,1,0:T(8,128)(2,1)S(1)}, bf16[4,256,1024]{2,1,0:T(8,128)(2,1)}, u32[]{:S(2)}, u32[]{:S(2)}) collective-permute-start(bf16[4,256,1024]{2,1,0:T(8,128)(2,1)S(1)} %all-to-all-done.refs_1_.refs_0_.refs_2_), channel_id=1, source_target_pairs={{0,4},{4,0},{1,5},{5,1},{2,6},{6,2},{3,7},{7,3},{8,12},{12,8},{9,1... | collective-permute-start | bytes 6291464 | tf_op jit(solution)/shard_map/ppermute | solution.py:1136
  39.0 11.3 %collective-permute-start.5 = (bf16[64,1536]{1,0:T(8,128)(2,1)}, bf16[64,1536]{1,0:T(8,128)(2,1)}, u32[]{:S(2)}, u32[]{:S(2)}) collective-permute-start(bf16[64,1536]{1,0:T(8,128)(2,1)} %get-tuple-element.126.refs_3_), channel_id=1, source_target_pairs={{0,16},{8,24},{16,0},{24,8},{1,17},{9,25},{17,1},{25,9},{2,18},{10... | collective-permute-start | bytes 589832 | tf_op jit(solution)/shard_map/ppermute | solution.py:1141
  41.1 37.5 %all-to-all-start.1 = ((bf16[4,64,2688]{2,1,0:T(8,128)(2,1)}), bf16[4,64,2688]{2,1,0:T(8,128)(2,1)S(1)}, u32[]{:S(2)}, u32[]{:S(2)}) async-start(bf16[4,64,2688]{2,1,0:T(8,128)(2,1)} %get-tuple-element.134), calls=%async_computation.1 | async-start | bytes 2752512 | tf_op jit(solution)/shard_map/all_to_all | solution.py:1222
  50.8 22.5 %collective-permute-start.13 = (bf16[64,4096]{1,0:T(8,128)(2,1)}, bf16[64,4096]{1,0:T(8,128)(2,1)S(1)}, u32[]{:S(2)}, u32[]{:S(2)}) collective-permute-start(bf16[64,4096]{1,0:T(8,128)(2,1)} %get-tuple-element.148.refs_9_), channel_id=1, source_target_pairs={{0,24},{8,16},{16,8},{24,0},{1,25},{9,17},{17,9},{25,1},{2,26},{10... | collective-permute-start | bytes 1572872 | tf_op jit(solution)/shard_map/ppermute | solution.py:1141
  52.2 24.8 %collective-permute-start.12 = (bf16[64,4096]{1,0:T(8,128)(2,1)}, bf16[64,4096]{1,0:T(8,128)(2,1)S(1)}, u32[]{:S(2)}, u32[]{:S(2)}) collective-permute-start(bf16[64,4096]{1,0:T(8,128)(2,1)} %get-tuple-element.148.refs_9_), channel_id=1, source_target_pairs={{0,16},{8,24},{16,0},{24,8},{1,17},{9,25},{17,1},{25,9},{2,18},{10... | collective-permute-start | bytes 1572872 | tf_op jit(solution)/shard_map/ppermute | solution.py:1141
  53.7 24.2 %collective-permute-start.11 = (bf16[64,4096]{1,0:T(8,128)(2,1)}, bf16[64,4096]{1,0:T(8,128)(2,1)}, u32[]{:S(2)}, u32[]{:S(2)}) collective-permute-start(bf16[64,4096]{1,0:T(8,128)(2,1)} %get-tuple-element.148.refs_9_), channel_id=1, source_target_pairs={{0,8},{8,0},{16,24},{24,16},{1,9},{9,1},{17,25},{25,17},{2,10},{10... | collective-permute-start | bytes 1572872 | tf_op jit(solution)/shard_map/ppermute | solution.py:1141
  78.6 22.2 %all-to-all-start.2 = ((bf16[4,256,512]{2,1,0:T(8,128)(2,1)}), bf16[4,256,512]{2,1,0:T(8,128)(2,1)}, u32[]{:S(2)}, u32[]{:S(2)}) async-start(bf16[4,256,512]{2,1,0:T(8,128)(2,1)} %get-tuple-element.140), calls=%async_computation.2 | async-start | bytes 2097152 | tf_op jit(solution)/shard_map/all_to_all | solution.py:1150
  83.0 17.8 %collective-permute-start.15 = (bf16[64,4096]{1,0:T(8,128)(2,1)S(1)}, bf16[64,4096]{1,0:T(8,128)(2,1)}, u32[]{:S(2)}, u32[]{:S(2)}) collective-permute-start(bf16[64,4096]{1,0:T(8,128)(2,1)S(1)} %copy-done.11), channel_id=1, source_target_pairs={{0,4},{4,0},{1,5},{5,1},{2,6},{6,2},{3,7},{7,3},{8,12},{12,8},{9,1... | collective-permute-start | bytes 1572872 | tf_op jit(solution)/shard_map/ppermute | solution.py:1136
  83.6 17.2 %collective-permute-start.16 = (bf16[64,4096]{1,0:T(8,128)(2,1)}, bf16[64,4096]{1,0:T(8,128)(2,1)}, u32[]{:S(2)}, u32[]{:S(2)}) collective-permute-start(bf16[64,4096]{1,0:T(8,128)(2,1)} %collective-permute-done.11.refs_10_), channel_id=1, source_target_pairs={{0,4},{4,0},{1,5},{5,1},{2,6},{6,2},{3,7},{7,3},{8,12},{12,8},{9,1... | collective-permute-start | bytes 1572872 | tf_op jit(solution)/shard_map/ppermute | solution.py:1136
  83.7 17.2 %collective-permute-start.17 = (bf16[64,4096]{1,0:T(8,128)(2,1)}, bf16[64,4096]{1,0:T(8,128)(2,1)}, u32[]{:S(2)}, u32[]{:S(2)}) collective-permute-start(bf16[64,4096]{1,0:T(8,128)(2,1)} %copy-done.13), channel_id=1, source_target_pairs={{0,4},{4,0},{1,5},{5,1},{2,6},{6,2},{3,7},{7,3},{8,12},{12,8},{9,1... | collective-permute-start | bytes 1572872 | tf_op jit(solution)/shard_map/ppermute | solution.py:1136
  84.1 16.7 %collective-permute-start.18 = (bf16[64,4096]{1,0:T(8,128)(2,1)}, bf16[64,4096]{1,0:T(8,128)(2,1)}, u32[]{:S(2)}, u32[]{:S(2)}) collective-permute-start(bf16[64,4096]{1,0:T(8,128)(2,1)} %copy-done.12), channel_id=1, source_target_pairs={{0,4},{4,0},{1,5},{5,1},{2,6},{6,2},{3,7},{7,3},{8,12},{12,8},{9,1... | collective-permute-start | bytes 1572872 | tf_op jit(solution)/shard_map/ppermute | solution.py:1136
  110.9 12.5 %all-to-all-start.3 = ((bf16[4,272,256]{2,1,0:T(8,128)(2,1)}), bf16[4,272,256]{2,1,0:T(8,128)(2,1)S(1)}, u32[]{:S(2)}, u32[]{:S(2)}) async-start(bf16[4,272,256]{2,1,0:T(8,128)(2,1)} %get-tuple-element.155), calls=%async_computation.3 | async-start | bytes 1114112 | tf_op jit(solution)/shard_map/all_to_all | solution.py:1150
  123.3 30.7 %collective-permute-start.19 = (bf16[4,256,512]{2,1,0:T(8,128)(2,1)}, bf16[4,256,512]{2,1,0:T(8,128)(2,1)}, u32[]{:S(2)}, u32[]{:S(2)}) collective-permute-start(bf16[4,256,512]{2,1,0:T(8,128)(2,1)} %all-to-all-done.2.refs_0_.refs_3_), channel_id=1, source_target_pairs={{0,4},{4,0},{1,5},{5,1},{2,6},{6,2},{3,7},{7,3},{8,12},{12,8},{9,1... | collective-permute-start | bytes 3145736 | tf_op jit(solution)/shard_map/ppermute | solution.py:1136
  124.1 39.5 %all-to-all-start.4 = ((bf16[4,128,2304]{2,1,0:T(8,128)(2,1)}), bf16[4,128,2304]{2,1,0:T(8,128)(2,1)S(1)}, u32[]{:S(2)}, u32[]{:S(2)}) async-start(bf16[4,128,2304]{2,1,0:T(8,128)(2,1)} %grads_a.1), calls=%async_computation.4 | async-start | bytes 4718592 | tf_op jit(solution)/shard_map/all_to_all | solution.py:1150
  173.0 34.5 %collective-permute-start.27 = (bf16[32,2816]{1,0:T(8,128)(2,1)}, bf16[32,2816]{1,0:T(8,128)(2,1)S(1)}, u32[]{:S(2)}, u32[]{:S(2)}) collective-permute-start(bf16[32,2816]{1,0:T(8,128)(2,1)} %get-tuple-element.200), channel_id=1, source_target_pairs={{0,1},{1,0},{2,3},{3,2},{4,5},{5,4},{6,7},{7,6},{8,9},{9,8},{10,11... | collective-permute-start | bytes 540680 | tf_op jit(solution)/shard_map/ppermute | solution.py:1146
  174.2 33.3 %collective-permute-start.28 = (bf16[32,2816]{1,0:T(8,128)(2,1)}, bf16[32,2816]{1,0:T(8,128)(2,1)S(1)}, u32[]{:S(2)}, u32[]{:S(2)}) collective-permute-start(bf16[32,2816]{1,0:T(8,128)(2,1)} %get-tuple-element.201), channel_id=1, source_target_pairs={{0,2},{1,3},{2,0},{3,1},{4,6},{5,7},{6,4},{7,5},{8,10},{9,11},{10,... | collective-permute-start | bytes 540680 | tf_op jit(solution)/shard_map/ppermute | solution.py:1146
  176.8 30.7 %collective-permute-start.29 = (bf16[32,2816]{1,0:T(8,128)(2,1)}, bf16[32,2816]{1,0:T(8,128)(2,1)S(1)}, u32[]{:S(2)}, u32[]{:S(2)}) collective-permute-start(bf16[32,2816]{1,0:T(8,128)(2,1)} %get-tuple-element.202), channel_id=1, source_target_pairs={{0,3},{1,2},{2,1},{3,0},{4,7},{5,6},{6,5},{7,4},{8,11},{9,10},{10,... | collective-permute-start | bytes 540680 | tf_op jit(solution)/shard_map/ppermute | solution.py:1146
  177.4 26.6 %all-to-all-start.6 = ((bf16[8,64,1664]{2,1,0:T(8,128)(2,1)}), bf16[8,64,1664]{2,1,0:T(8,128)(2,1)S(1)}, u32[]{:S(2)}, u32[]{:S(2)}) async-start(bf16[8,64,1664]{2,1,0:T(8,128)(2,1)} %grads_b.1), calls=%async_computation.6 | async-start | bytes 3407872 | tf_op jit(solution)/shard_map/all_to_all | solution.py:1154
  207.6 22.0 %all-to-all-start.7 = ((bf16[8,192,256]{2,1,0:T(8,128)(2,1)}), bf16[8,192,256]{2,1,0:T(8,128)(2,1)S(1)}, u32[]{:S(2)}, u32[]{:S(2)}) async-start(bf16[8,192,256]{2,1,0:T(8,128)(2,1)} %pair_back.3.refs_0_), calls=%async_computation.7 | async-start | bytes 1572864 | tf_op jit(solution)/shard_map/all_to_all | solution.py:1154
  211.5 11.0 %collective-permute-start.31 = (bf16[16,2816]{1,0:T(8,128)(2,1)}, bf16[16,2816]{1,0:T(8,128)(2,1)S(1)}, u32[]{:S(2)}, u32[]{:S(2)}) collective-permute-start(bf16[16,2816]{1,0:T(8,128)(2,1)} %get-tuple-element.210), channel_id=1, source_target_pairs={{0,2},{1,3},{2,0},{3,1},{4,6},{5,7},{6,4},{7,5},{8,10},{9,11},{10,... | collective-permute-start | bytes 270344 | tf_op jit(solution)/shard_map/ppermute | solution.py:1146
  (65 other events, 288.9 us)
